TPU v7x, 128 devices: a whole 4x4x4 slice. The times are simulated.
128 devices in a mesh: axial: 32 (over y, x, core), theta: 4 (over z).
Axes of the slice: x: 4, y: 4, z: 4, core: 2. Of those that a mesh axis runs over, the one named last changes fastest.
Arguments:
- rhs_field: float32 [16, 64, 32, 320], P('theta', 'axial'), may hold values from -6 to 6
- diag_inv: float32 [16, 64, 320, 320], P('theta', 'axial'), may hold values from -0.5 to 2
- lower_block: float32 [16, 64, 320, 320], P('theta', 'axial'), may hold values from -2 to 0.5
- upper_block: float32 [16, 64, 320, 320], P('theta', 'axial'), may hold values from -2 to 0.5
- proj_table: float32 [16, 80, 80], replicated, may hold values from -0.5 to 0.5
- intersection_list: int32 [16, 2], P('theta'), may hold values from 0 to 15
- proj_index: int32 [16, 2], P('theta'), may hold values from 0 to 15
- angle_step: int32 [1], replicated, may hold values from 0 to 15
Outputs:
- solution: float32 [16, 64, 32, 320], P('theta', 'axial')
- mortar: float32 [32, 16, 2560], P('axial', 'theta')
All inputs are finite; a program needn't handle non-finite values.
Results may differ from a plain program's by a relative error of at most 0.0002.
Values sent between devices are 32-bit elements; how exact they have to be, the bound alone decides.
A program may use at most 64 MiB of HBM per device.

v0:
```python
import jax
import jax.numpy as jnp
from jax import lax
from jax.sharding import PartitionSpec as P


def shifted(value, axis, steps):
    count = lax.axis_size(axis)
    first, last = (max(0, -steps), min(count, count - steps))
    return lax.ppermute(value, axis, [(source, source + steps) for source in range(first, last)])


def product(blocks, vectors):
    return jnp.einsum("lbc,lvc->lvb", blocks, vectors, precision=lax.Precision.HIGHEST)


def forward_lines(rhs_part, inverse_part, lower_part, incoming):
    previous = incoming
    results = []
    for element in range(rhs_part.shape[1]):
        inner = rhs_part[:, element] - product(lower_part[:, element], previous)
        previous = product(inverse_part[:, element], inner)
        results.append(previous)
    return jnp.stack(results, axis=1)


def backward_lines(swept_part, inverse_part, upper_part, incoming):
    following = incoming
    results = []
    for element in reversed(range(swept_part.shape[1])):
        coupled = product(upper_part[:, element], following)
        following = swept_part[:, element] - product(inverse_part[:, element], coupled)
        results.append(following)
    return jnp.stack(results[::-1], axis=1)


def run_forward(rhs_field, diag_inv, lower_block, group_size):
    batch_total = rhs_field.shape[0] // group_size
    chain_size = lax.axis_size("axial")
    position = lax.axis_index("axial")
    boundary = jnp.zeros((group_size,) + rhs_field.shape[2:], jnp.float32)

    def advance(section_no, carried):
        result, incoming = carried
        batch_id = section_no - position
        active = jnp.logical_and(batch_id >= 0, batch_id < batch_total)
        offset = jnp.clip(batch_id, 0, batch_total - 1) * group_size

        def window(source):
            return source

        def working(current):
            values = forward_lines(
                window(rhs_field), window(diag_inv), window(lower_block), incoming
            )
            return (lax.dynamic_update_slice_in_dim(current, values, offset, 0), values[:, -1])

        def waiting(current):
            return (current, boundary)

        result, edge_values = lax.cond(active, working, waiting, result)
        outgoing = shifted(edge_values, "axial", 1)
        return (result, outgoing)

    result, _ = lax.fori_loop(
        0, chain_size + batch_total - 1, advance, (jnp.zeros_like(rhs_field), boundary)
    )
    return result


def run_backward(swept, diag_inv, upper_block, group_size):
    batch_total = swept.shape[0] // group_size
    chain_size = lax.axis_size("axial")
    position = chain_size - 1 - lax.axis_index("axial")
    boundary = jnp.zeros((group_size,) + swept.shape[2:], jnp.float32)

    def advance(section_no, carried):
        result, incoming = carried
        batch_id = section_no - position
        active = jnp.logical_and(batch_id >= 0, batch_id < batch_total)
        offset = jnp.clip(batch_id, 0, batch_total - 1) * group_size

        def window(source):
            return source

        def working(current):
            values = backward_lines(window(swept), window(diag_inv), window(upper_block), incoming)
            return (lax.dynamic_update_slice_in_dim(current, values, offset, 0), values[:, 0])

        def waiting(current):
            return (current, boundary)

        result, edge_values = lax.cond(active, working, waiting, result)
        outgoing = shifted(edge_values, "axial", -1)
        return (result, outgoing)

    result, _ = lax.fori_loop(
        0, chain_size + batch_total - 1, advance, (jnp.zeros_like(swept), boundary)
    )
    return result


def local(
    rhs_field,
    diag_inv,
    lower_block,
    upper_block,
    proj_table,
    intersection_list,
    proj_index,
    angle_step,
):
    lines_here = rhs_field.shape[0]
    swept = run_forward(rhs_field, diag_inv, lower_block, lines_here)
    solution = run_backward(swept, diag_inv, upper_block, lines_here)
    face_size = proj_table.shape[1]
    vec_count = rhs_field.shape[2]
    block_size = rhs_field.shape[3]
    intersection_count = intersection_list.shape[1]
    traces = solution[:, -1, :, block_size - face_size :].reshape(lines_here, vec_count * face_size)
    total_lines = lines_here * lax.axis_size("theta")
    sources = (intersection_list + angle_step[0]) % total_lines
    segment = lax.all_gather(traces, "theta", axis=0, tiled=True)
    row_ids = jnp.arange(segment.shape[0], dtype=jnp.int32)
    select = (sources[:, :, None] == row_ids[None, None, :]).astype(jnp.float32)
    picked = jnp.einsum("lkn,nw->lkw", select, segment, precision=lax.Precision.HIGHEST)
    one_hot = jax.nn.one_hot(proj_index, proj_table.shape[0], dtype=jnp.float32)
    chosen = jnp.einsum("gkp,pfh->gkfh", one_hot, proj_table, precision=lax.Precision.HIGHEST)
    picked = picked.reshape(lines_here, intersection_count, vec_count, face_size)
    mortar = jnp.einsum("gkfh,gkvh->gvf", chosen, picked, precision=lax.Precision.HIGHEST)
    return (solution, mortar.reshape(1, lines_here, vec_count * face_size))


def solution(mesh):
    return jax.shard_map(
        local,
        mesh=mesh,
        in_specs=(
            P("theta", "axial", None, None),
            P("theta", "axial", None, None),
            P("theta", "axial", None, None),
            P("theta", "axial", None, None),
            P(),
            P("theta", None),
            P("theta", None),
            P(),
        ),
        out_specs=(P("theta", "axial", None, None), P("axial", "theta", None)),
        check_vma=False,
    )
```

profile of v0, /device:TPU:1, one launch (start us, length us, event | category | flops | bytes accessed | tf_op | source)
XLA Modules:
  0.0 1233.8 jit_solution(249738860508706743)
XLA Ops:
  5.1 411.4 %while.36 = (s32[]{:T(128)}, f32[4,2,32,320]{3,2,0,1:T(8,128)S(1)}, f32[4,32,320]{2,1,0:T(8,128)S(1)}, s32[]{:T(128)}, f32[4,2,32,320]{3,2,0,1:T(8,128)S(1)}, /*...) while((s32[]{:T(128)}, f32[4,2,32,320]{3,2,0,1:T(8,128)S(1)}, ...), condition=%wide.region_3.4_spmd, body=%wide.region_0.3_spmd.sunk | while | flops 629309440 | bytes 23953656 | solution.py:65
  10.3 12.8 %collective-permute-done = f32[4,32,320]{2,1,0:T(8,128)S(1)} collective-permute-done((f32[4,32,320]{2,1,0:T(8,128)}, f32[4,32,320]{2,1,0:T(8,128)S(1)}, u32[]{:S(2)}, u32[]{:S(2)}) %collective-permute-start) | collective-permute-done | bytes 163872 | tf_op jit(solution)/shard_map/while/body/eval_jaxpr/ppermute | solution.py:10
  23.1 14.1 %conditional.4 = (f32[4,2,32,320]{3,2,0,1:T(8,128)S(1)}, f32[4,32,320]{2,1,0:T(8,128)}) conditional(s32[]{:T(128)} %convert_element_type.19, f32[4,2,32,320]{3,2,0,1:T(8,128)S(1)} %get-tuple-element.478, (f32[4,2,32,320]{3,2,0,1:T(8,128)S(1)}, f32[4,2,320,320]{3,2,1,0:T(8,128)}, f32[4,32,320]{2,1,0:T(8,128)S(1)}, f32[4,2,320,320]{3,2,0,1:T(8,128)}) %tuple.90), branch_computations={%region_1.1_spmd, %region_2.2_spmd} | conditional | flops 629309440 | bytes 23298092 | solution.py:61
  42.8 17.7 %collective-permute-start = (f32[4,32,320]{2,1,0:T(8,128)}, f32[4,32,320]{2,1,0:T(8,128)S(1)}, u32[]{:S(2)}, u32[]{:S(2)}) collective-permute-start(f32[4,32,320]{2,1,0:T(8,128)} %get-tuple-element.450), channel_id=1, source_target_pairs={{0,4},{4,8},{8,12},{12,16},{16,20},{20,24},{24,28},{28,32},{32,36}... | collective-permute-start | bytes 491528 | tf_op jit(solution)/shard_map/while/body/eval_jaxpr/ppermute | solution.py:10
  72.0 10.1 collective-permute-start
  93.6 15.4 %collective-permute-start = (f32[4,32,320]{2,1,0:T(8,128)}, f32[4,32,320]{2,1,0:T(8,128)S(1)}, u32[]{:S(2)}, u32[]{:S(2)}) collective-permute-start(f32[4,32,320]{2,1,0:T(8,128)} %get-tuple-element.450), channel_id=1, source_target_pairs={{0,4},{4,8},{8,12},{12,16},{16,20},{20,24},{24,28},{28,32},{32,36}... | collective-permute-start | bytes 491528 | tf_op jit(solution)/shard_map/while/body/eval_jaxpr/ppermute | solution.py:10
  120.4 10.1 collective-permute-start
  142.0 15.4 %collective-permute-start = (f32[4,32,320]{2,1,0:T(8,128)}, f32[4,32,320]{2,1,0:T(8,128)S(1)}, u32[]{:S(2)}, u32[]{:S(2)}) collective-permute-start(f32[4,32,320]{2,1,0:T(8,128)} %get-tuple-element.450), channel_id=1, source_target_pairs={{0,4},{4,8},{8,12},{12,16},{16,20},{20,24},{24,28},{28,32},{32,36}... | collective-permute-start | bytes 491528 | tf_op jit(solution)/shard_map/while/body/eval_jaxpr/ppermute | solution.py:10
  168.8 10.1 collective-permute-start
  190.4 17.5 %collective-permute-start = (f32[4,32,320]{2,1,0:T(8,128)}, f32[4,32,320]{2,1,0:T(8,128)S(1)}, u32[]{:S(2)}, u32[]{:S(2)}) collective-permute-start(f32[4,32,320]{2,1,0:T(8,128)} %get-tuple-element.450), channel_id=1, source_target_pairs={{0,4},{4,8},{8,12},{12,16},{16,20},{20,24},{24,28},{28,32},{32,36}... | collective-permute-start | bytes 491528 | tf_op jit(solution)/shard_map/while/body/eval_jaxpr/ppermute | solution.py:10
  221.4 8.0 collective-permute-start
  243.0 13.3 %collective-permute-start = (f32[4,32,320]{2,1,0:T(8,128)}, f32[4,32,320]{2,1,0:T(8,128)S(1)}, u32[]{:S(2)}, u32[]{:S(2)}) collective-permute-start(f32[4,32,320]{2,1,0:T(8,128)} %get-tuple-element.450), channel_id=1, source_target_pairs={{0,4},{4,8},{8,12},{12,16},{16,20},{20,24},{24,28},{28,32},{32,36}... | collective-permute-start | bytes 491528 | tf_op jit(solution)/shard_map/while/body/eval_jaxpr/ppermute | solution.py:10
  269.8 8.0 collective-permute-start
  291.4 13.3 %collective-permute-start = (f32[4,32,320]{2,1,0:T(8,128)}, f32[4,32,320]{2,1,0:T(8,128)S(1)}, u32[]{:S(2)}, u32[]{:S(2)}) collective-permute-start(f32[4,32,320]{2,1,0:T(8,128)} %get-tuple-element.450), channel_id=1, source_target_pairs={{0,4},{4,8},{8,12},{12,16},{16,20},{20,24},{24,28},{28,32},{32,36}... | collective-permute-start | bytes 491528 | tf_op jit(solution)/shard_map/while/body/eval_jaxpr/ppermute | solution.py:10
  318.2 8.0 collective-permute-start
  339.8 13.3 %collective-permute-start = (f32[4,32,320]{2,1,0:T(8,128)}, f32[4,32,320]{2,1,0:T(8,128)S(1)}, u32[]{:S(2)}, u32[]{:S(2)}) collective-permute-start(f32[4,32,320]{2,1,0:T(8,128)} %get-tuple-element.450), channel_id=1, source_target_pairs={{0,4},{4,8},{8,12},{12,16},{16,20},{20,24},{24,28},{28,32},{32,36}... | collective-permute-start | bytes 491528 | tf_op jit(solution)/shard_map/while/body/eval_jaxpr/ppermute | solution.py:10
  366.6 8.0 collective-permute-start
  388.2 15.4 %collective-permute-start = (f32[4,32,320]{2,1,0:T(8,128)}, f32[4,32,320]{2,1,0:T(8,128)S(1)}, u32[]{:S(2)}, u32[]{:S(2)}) collective-permute-start(f32[4,32,320]{2,1,0:T(8,128)} %get-tuple-element.450), channel_id=1, source_target_pairs={{0,4},{4,8},{8,12},{12,16},{16,20},{20,24},{24,28},{28,32},{32,36}... | collective-permute-start | bytes 491528 | tf_op jit(solution)/shard_map/while/body/eval_jaxpr/ppermute | solution.py:10
  416.5 802.6 %while.37 = (s32[]{:T(128)}, f32[4,2,32,320]{3,2,0,1:T(8,128)S(1)}, f32[4,32,320]{2,1,0:T(8,128)S(1)}, s32[]{:T(128)}, f32[4,2,32,320]{3,2,0,1:T(8,128)S(1)}, /*...) while((s32[]{:T(128)}, f32[4,2,32,320]{3,2,0,1:T(8,128)S(1)}, ...), condition=%wide.region_7.8_spmd, body=%wide.region_4.7_spmd.sunk | while | flops 629309440 | bytes 23986424 | solution.py:97
  419.4 9.6 collective-permute-done.1
  441.4 14.9 %collective-permute-done.1 = f32[4,32,320]{2,1,0:T(8,128)S(1)} collective-permute-done((f32[4,32,320]{2,1,0:T(8,128)}, f32[4,32,320]{2,1,0:T(8,128)S(1)}, u32[]{:S(2)}, u32[]{:S(2)}) %collective-permute-start.1) | collective-permute-done | bytes 163872 | tf_op jit(solution)/shard_map/while/body/eval_jaxpr/ppermute | solution.py:10
  468.8 9.6 collective-permute-done.1
  490.9 14.9 %collective-permute-done.1 = f32[4,32,320]{2,1,0:T(8,128)S(1)} collective-permute-done((f32[4,32,320]{2,1,0:T(8,128)}, f32[4,32,320]{2,1,0:T(8,128)S(1)}, u32[]{:S(2)}, u32[]{:S(2)}) %collective-permute-start.1) | collective-permute-done | bytes 163872 | tf_op jit(solution)/shard_map/while/body/eval_jaxpr/ppermute | solution.py:10
  508.4 7.4 collective-permute-done.1
  518.4 9.5 collective-permute-done.1
  530.4 7.4 collective-permute-done.1
  540.4 14.8 %collective-permute-done.1 = f32[4,32,320]{2,1,0:T(8,128)S(1)} collective-permute-done((f32[4,32,320]{2,1,0:T(8,128)}, f32[4,32,320]{2,1,0:T(8,128)S(1)}, u32[]{:S(2)}, u32[]{:S(2)}) %collective-permute-start.1) | collective-permute-done | bytes 163872 | tf_op jit(solution)/shard_map/while/body/eval_jaxpr/ppermute | solution.py:10
  557.8 7.4 collective-permute-done.1
  567.8 9.5 collective-permute-done.1
  579.9 7.4 collective-permute-done.1
  589.9 16.9 %collective-permute-done.1 = f32[4,32,320]{2,1,0:T(8,128)S(1)} collective-permute-done((f32[4,32,320]{2,1,0:T(8,128)}, f32[4,32,320]{2,1,0:T(8,128)S(1)}, u32[]{:S(2)}, u32[]{:S(2)}) %collective-permute-start.1) | collective-permute-done | bytes 163872 | tf_op jit(solution)/shard_map/while/body/eval_jaxpr/ppermute | solution.py:10
  609.4 7.4 collective-permute-done.1
  619.3 9.5 collective-permute-done.1
  631.4 7.4 collective-permute-done.1
  641.4 14.8 %collective-permute-done.1 = f32[4,32,320]{2,1,0:T(8,128)S(1)} collective-permute-done((f32[4,32,320]{2,1,0:T(8,128)}, f32[4,32,320]{2,1,0:T(8,128)S(1)}, u32[]{:S(2)}, u32[]{:S(2)}) %collective-permute-start.1) | collective-permute-done | bytes 163872 | tf_op jit(solution)/shard_map/while/body/eval_jaxpr/ppermute | solution.py:10
  658.8 7.4 collective-permute-done.1
  668.8 9.5 collective-permute-done.1
  680.9 7.4 collective-permute-done.1
  690.8 14.8 %collective-permute-done.1 = f32[4,32,320]{2,1,0:T(8,128)S(1)} collective-permute-done((f32[4,32,320]{2,1,0:T(8,128)}, f32[4,32,320]{2,1,0:T(8,128)S(1)}, u32[]{:S(2)}, u32[]{:S(2)}) %collective-permute-start.1) | collective-permute-done | bytes 163872 | tf_op jit(solution)/shard_map/while/body/eval_jaxpr/ppermute | solution.py:10
  708.2 7.4 collective-permute-done.1
  718.2 9.5 collective-permute-done.1
  730.3 7.4 collective-permute-done.1
  740.3 14.8 %collective-permute-done.1 = f32[4,32,320]{2,1,0:T(8,128)S(1)} collective-permute-done((f32[4,32,320]{2,1,0:T(8,128)}, f32[4,32,320]{2,1,0:T(8,128)S(1)}, u32[]{:S(2)}, u32[]{:S(2)}) %collective-permute-start.1) | collective-permute-done | bytes 163872 | tf_op jit(solution)/shard_map/while/body/eval_jaxpr/ppermute | solution.py:10
  767.6 9.5 collective-permute-done.1
  779.7 404.4 %collective-permute-done.1 = f32[4,32,320]{2,1,0:T(8,128)S(1)} collective-permute-done((f32[4,32,320]{2,1,0:T(8,128)}, f32[4,32,320]{2,1,0:T(8,128)S(1)}, u32[]{:S(2)}, u32[]{:S(2)}) %collective-permute-start.1) | collective-permute-done | bytes 163872 | tf_op jit(solution)/shard_map/while/body/eval_jaxpr/ppermute | solution.py:10
  1184.2 14.1 %conditional.5 = (f32[4,2,32,320]{3,2,0,1:T(8,128)S(1)}, f32[4,32,320]{2,1,0:T(8,128)}) conditional(s32[]{:T(128)} %convert_element_type.20, f32[4,2,32,320]{3,2,0,1:T(8,128)S(1)} %get-tuple-element.505, (f32[4,2,32,320]{3,2,0,1:T(8,128)S(1)}, f32[4,2,320,320]{3,2,1,0:T(8,128)}, f32[4,32,320]{2,1,0:T(8,128)S(1)}, f32[4,2,320,320]{3,2,0,1:T(8,128)}) %tuple.92), branch_computations={%region_5.5_spmd, %region_6.6_spmd} | conditional | flops 629309440 | bytes 23330860 | solution.py:93
  1206.2 11.7 collective-permute-start.1
  1219.4 10.6 all-gather
  (248 shorter events, 396.0 us)
Async XLA Ops:
  5.8 17.3 %collective-permute-start = (f32[4,32,320]{2,1,0:T(8,128)}, f32[4,32,320]{2,1,0:T(8,128)S(1)}, u32[]{:S(2)}, u32[]{:S(2)}) collective-permute-start(f32[4,32,320]{2,1,0:T(8,128)} %get-tuple-element.450), channel_id=1, source_target_pairs={{0,4},{4,8},{8,12},{12,16},{16,20},{20,24},{24,28},{28,32},{32,36}... | collective-permute-start | bytes 491528 | tf_op jit(solution)/shard_map/while/body/eval_jaxpr/ppermute | solution.py:10
  42.8 20.6 %collective-permute-start = (f32[4,32,320]{2,1,0:T(8,128)}, f32[4,32,320]{2,1,0:T(8,128)S(1)}, u32[]{:S(2)}, u32[]{:S(2)}) collective-permute-start(f32[4,32,320]{2,1,0:T(8,128)} %get-tuple-element.450), channel_id=1, source_target_pairs={{0,4},{4,8},{8,12},{12,16},{16,20},{20,24},{24,28},{28,32},{32,36}... | collective-permute-start | bytes 491528 | tf_op jit(solution)/shard_map/while/body/eval_jaxpr/ppermute | solution.py:10
  72.0 13.0 %collective-permute-start = (f32[4,32,320]{2,1,0:T(8,128)}, f32[4,32,320]{2,1,0:T(8,128)S(1)}, u32[]{:S(2)}, u32[]{:S(2)}) collective-permute-start(f32[4,32,320]{2,1,0:T(8,128)} %get-tuple-element.450), channel_id=1, source_target_pairs={{0,4},{4,8},{8,12},{12,16},{16,20},{20,24},{24,28},{28,32},{32,36}... | collective-permute-start | bytes 491528 | tf_op jit(solution)/shard_map/while/body/eval_jaxpr/ppermute | solution.py:10
  93.6 18.3 %collective-permute-start = (f32[4,32,320]{2,1,0:T(8,128)}, f32[4,32,320]{2,1,0:T(8,128)S(1)}, u32[]{:S(2)}, u32[]{:S(2)}) collective-permute-start(f32[4,32,320]{2,1,0:T(8,128)} %get-tuple-element.450), channel_id=1, source_target_pairs={{0,4},{4,8},{8,12},{12,16},{16,20},{20,24},{24,28},{28,32},{32,36}... | collective-permute-start | bytes 491528 | tf_op jit(solution)/shard_map/while/body/eval_jaxpr/ppermute | solution.py:10
  120.4 13.0 %collective-permute-start = (f32[4,32,320]{2,1,0:T(8,128)}, f32[4,32,320]{2,1,0:T(8,128)S(1)}, u32[]{:S(2)}, u32[]{:S(2)}) collective-permute-start(f32[4,32,320]{2,1,0:T(8,128)} %get-tuple-element.450), channel_id=1, source_target_pairs={{0,4},{4,8},{8,12},{12,16},{16,20},{20,24},{24,28},{28,32},{32,36}... | collective-permute-start | bytes 491528 | tf_op jit(solution)/shard_map/while/body/eval_jaxpr/ppermute | solution.py:10
  142.0 18.3 %collective-permute-start = (f32[4,32,320]{2,1,0:T(8,128)}, f32[4,32,320]{2,1,0:T(8,128)S(1)}, u32[]{:S(2)}, u32[]{:S(2)}) collective-permute-start(f32[4,32,320]{2,1,0:T(8,128)} %get-tuple-element.450), channel_id=1, source_target_pairs={{0,4},{4,8},{8,12},{12,16},{16,20},{20,24},{24,28},{28,32},{32,36}... | collective-permute-start | bytes 491528 | tf_op jit(solution)/shard_map/while/body/eval_jaxpr/ppermute | solution.py:10
  168.8 13.0 %collective-permute-start = (f32[4,32,320]{2,1,0:T(8,128)}, f32[4,32,320]{2,1,0:T(8,128)S(1)}, u32[]{:S(2)}, u32[]{:S(2)}) collective-permute-start(f32[4,32,320]{2,1,0:T(8,128)} %get-tuple-element.450), channel_id=1, source_target_pairs={{0,4},{4,8},{8,12},{12,16},{16,20},{20,24},{24,28},{28,32},{32,36}... | collective-permute-start | bytes 491528 | tf_op jit(solution)/shard_map/while/body/eval_jaxpr/ppermute | solution.py:10
  190.4 20.4 %collective-permute-start = (f32[4,32,320]{2,1,0:T(8,128)}, f32[4,32,320]{2,1,0:T(8,128)S(1)}, u32[]{:S(2)}, u32[]{:S(2)}) collective-permute-start(f32[4,32,320]{2,1,0:T(8,128)} %get-tuple-element.450), channel_id=1, source_target_pairs={{0,4},{4,8},{8,12},{12,16},{16,20},{20,24},{24,28},{28,32},{32,36}... | collective-permute-start | bytes 491528 | tf_op jit(solution)/shard_map/while/body/eval_jaxpr/ppermute | solution.py:10
  211.4 9.3 collective-permute-start
  221.4 10.9 collective-permute-start
  233.0 9.3 collective-permute-start
  243.0 16.2 %collective-permute-start = (f32[4,32,320]{2,1,0:T(8,128)}, f32[4,32,320]{2,1,0:T(8,128)S(1)}, u32[]{:S(2)}, u32[]{:S(2)}) collective-permute-start(f32[4,32,320]{2,1,0:T(8,128)} %get-tuple-element.450), channel_id=1, source_target_pairs={{0,4},{4,8},{8,12},{12,16},{16,20},{20,24},{24,28},{28,32},{32,36}... | collective-permute-start | bytes 491528 | tf_op jit(solution)/shard_map/while/body/eval_jaxpr/ppermute | solution.py:10
  259.8 9.3 collective-permute-start
  269.8 10.9 collective-permute-start
  281.4 9.3 collective-permute-start
  291.4 16.2 %collective-permute-start = (f32[4,32,320]{2,1,0:T(8,128)}, f32[4,32,320]{2,1,0:T(8,128)S(1)}, u32[]{:S(2)}, u32[]{:S(2)}) collective-permute-start(f32[4,32,320]{2,1,0:T(8,128)} %get-tuple-element.450), channel_id=1, source_target_pairs={{0,4},{4,8},{8,12},{12,16},{16,20},{20,24},{24,28},{28,32},{32,36}... | collective-permute-start | bytes 491528 | tf_op jit(solution)/shard_map/while/body/eval_jaxpr/ppermute | solution.py:10
  308.2 9.3 collective-permute-start
  318.2 10.9 collective-permute-start
  329.8 9.3 collective-permute-start
  339.8 16.2 %collective-permute-start = (f32[4,32,320]{2,1,0:T(8,128)}, f32[4,32,320]{2,1,0:T(8,128)S(1)}, u32[]{:S(2)}, u32[]{:S(2)}) collective-permute-start(f32[4,32,320]{2,1,0:T(8,128)} %get-tuple-element.450), channel_id=1, source_target_pairs={{0,4},{4,8},{8,12},{12,16},{16,20},{20,24},{24,28},{28,32},{32,36}... | collective-permute-start | bytes 491528 | tf_op jit(solution)/shard_map/while/body/eval_jaxpr/ppermute | solution.py:10
  356.7 9.3 collective-permute-start
  366.6 10.9 collective-permute-start
  378.2 9.3 collective-permute-start
  388.2 18.3 %collective-permute-start = (f32[4,32,320]{2,1,0:T(8,128)}, f32[4,32,320]{2,1,0:T(8,128)S(1)}, u32[]{:S(2)}, u32[]{:S(2)}) collective-permute-start(f32[4,32,320]{2,1,0:T(8,128)} %get-tuple-element.450), channel_id=1, source_target_pairs={{0,4},{4,8},{8,12},{12,16},{16,20},{20,24},{24,28},{28,32},{32,36}... | collective-permute-start | bytes 491528 | tf_op jit(solution)/shard_map/while/body/eval_jaxpr/ppermute | solution.py:10
  407.2 9.3 collective-permute-start
  417.4 11.5 collective-permute-start.1
  439.5 16.8 %collective-permute-start.1 = (f32[4,32,320]{2,1,0:T(8,128)}, f32[4,32,320]{2,1,0:T(8,128)S(1)}, u32[]{:S(2)}, u32[]{:S(2)}) collective-permute-start(f32[4,32,320]{2,1,0:T(8,128)} %get-tuple-element.459), channel_id=1, source_target_pairs={{4,0},{8,4},{12,8},{16,12},{20,16},{24,20},{28,24},{32,28},{36,32}... | collective-permute-start | bytes 491528 | tf_op jit(solution)/shard_map/while/body/eval_jaxpr/ppermute | solution.py:10
  466.9 11.5 collective-permute-start.1
  489.0 16.8 %collective-permute-start.1 = (f32[4,32,320]{2,1,0:T(8,128)}, f32[4,32,320]{2,1,0:T(8,128)S(1)}, u32[]{:S(2)}, u32[]{:S(2)}) collective-permute-start(f32[4,32,320]{2,1,0:T(8,128)} %get-tuple-element.459), channel_id=1, source_target_pairs={{4,0},{8,4},{12,8},{16,12},{20,16},{24,20},{28,24},{32,28},{36,32}... | collective-permute-start | bytes 491528 | tf_op jit(solution)/shard_map/while/body/eval_jaxpr/ppermute | solution.py:10
  506.5 9.3 collective-permute-start.1
  516.4 11.4 collective-permute-start.1
  528.5 9.3 collective-permute-start.1
  538.5 16.7 %collective-permute-start.1 = (f32[4,32,320]{2,1,0:T(8,128)}, f32[4,32,320]{2,1,0:T(8,128)S(1)}, u32[]{:S(2)}, u32[]{:S(2)}) collective-permute-start(f32[4,32,320]{2,1,0:T(8,128)} %get-tuple-element.459), channel_id=1, source_target_pairs={{4,0},{8,4},{12,8},{16,12},{20,16},{24,20},{28,24},{32,28},{36,32}... | collective-permute-start | bytes 491528 | tf_op jit(solution)/shard_map/while/body/eval_jaxpr/ppermute | solution.py:10
  565.9 11.4 collective-permute-start.1
  578.0 9.3 collective-permute-start.1
  587.9 18.8 %collective-permute-start.1 = (f32[4,32,320]{2,1,0:T(8,128)}, f32[4,32,320]{2,1,0:T(8,128)S(1)}, u32[]{:S(2)}, u32[]{:S(2)}) collective-permute-start(f32[4,32,320]{2,1,0:T(8,128)} %get-tuple-element.459), channel_id=1, source_target_pairs={{4,0},{8,4},{12,8},{16,12},{20,16},{24,20},{28,24},{32,28},{36,32}... | collective-permute-start | bytes 491528 | tf_op jit(solution)/shard_map/while/body/eval_jaxpr/ppermute | solution.py:10
  607.4 9.3 collective-permute-start.1
  617.4 11.4 collective-permute-start.1
  639.5 16.7 %collective-permute-start.1 = (f32[4,32,320]{2,1,0:T(8,128)}, f32[4,32,320]{2,1,0:T(8,128)S(1)}, u32[]{:S(2)}, u32[]{:S(2)}) collective-permute-start(f32[4,32,320]{2,1,0:T(8,128)} %get-tuple-element.459), channel_id=1, source_target_pairs={{4,0},{8,4},{12,8},{16,12},{20,16},{24,20},{28,24},{32,28},{36,32}... | collective-permute-start | bytes 491528 | tf_op jit(solution)/shard_map/while/body/eval_jaxpr/ppermute | solution.py:10
  666.9 11.4 collective-permute-start.1
  678.9 9.3 collective-permute-start.1
  688.9 16.7 %collective-permute-start.1 = (f32[4,32,320]{2,1,0:T(8,128)}, f32[4,32,320]{2,1,0:T(8,128)S(1)}, u32[]{:S(2)}, u32[]{:S(2)}) collective-permute-start(f32[4,32,320]{2,1,0:T(8,128)} %get-tuple-element.459), channel_id=1, source_target_pairs={{4,0},{8,4},{12,8},{16,12},{20,16},{24,20},{28,24},{32,28},{36,32}... | collective-permute-start | bytes 491528 | tf_op jit(solution)/shard_map/while/body/eval_jaxpr/ppermute | solution.py:10
  716.3 11.4 collective-permute-start.1
  728.4 9.3 collective-permute-start.1
  738.4 16.7 %collective-permute-start.1 = (f32[4,32,320]{2,1,0:T(8,128)}, f32[4,32,320]{2,1,0:T(8,128)S(1)}, u32[]{:S(2)}, u32[]{:S(2)}) collective-permute-start(f32[4,32,320]{2,1,0:T(8,128)} %get-tuple-element.459), channel_id=1, source_target_pairs={{4,0},{8,4},{12,8},{16,12},{20,16},{24,20},{28,24},{32,28},{36,32}... | collective-permute-start | bytes 491528 | tf_op jit(solution)/shard_map/while/body/eval_jaxpr/ppermute | solution.py:10
  765.7 11.4 collective-permute-start.1
  777.8 406.4 %collective-permute-start.1 = (f32[4,32,320]{2,1,0:T(8,128)}, f32[4,32,320]{2,1,0:T(8,128)S(1)}, u32[]{:S(2)}, u32[]{:S(2)}) collective-permute-start(f32[4,32,320]{2,1,0:T(8,128)} %get-tuple-element.459), channel_id=1, source_target_pairs={{4,0},{8,4},{12,8},{16,12},{20,16},{24,20},{28,24},{32,28},{36,32}... | collective-permute-start | bytes 491528 | tf_op jit(solution)/shard_map/while/body/eval_jaxpr/ppermute | solution.py:10
  1206.2 13.0 %collective-permute-start.1 = (f32[4,32,320]{2,1,0:T(8,128)}, f32[4,32,320]{2,1,0:T(8,128)S(1)}, u32[]{:S(2)}, u32[]{:S(2)}) collective-permute-start(f32[4,32,320]{2,1,0:T(8,128)} %get-tuple-element.459), channel_id=1, source_target_pairs={{4,0},{8,4},{12,8},{16,12},{20,16},{24,20},{28,24},{32,28},{36,32}... | collective-permute-start | bytes 491528 | tf_op jit(solution)/shard_map/while/body/eval_jaxpr/ppermute | solution.py:10
  (22 other events, 3013.9 us)
where the time goes:
time: 1240 us; the launch traced here: 1230 us
  waiting for transfers between devices  798 us (64%)
  starting transfers between devices  343 us (28%)
  local copies, waits for them, and re-layouts  49.3 us (4%)
  matrix products  27.6 us (2%)
    ppermute x64, waiting for transfers between devices, shifted(): lax.ppermute(value, axis, [(source, source + steps) for source in range(f...  798 us
    ppermute x64, starting transfers between devices, shifted(): lax.ppermute(value, axis, [(source, source + steps) for source in range(f...  343 us
    another operation x66, local copies, waits for them, and re-layouts  42.9 us
    dot_general x8, matrix products, product(): jnp.einsum('lbc,lvc->lvb', blocks, vectors, precision=lax.Precision.HIGHEST)  26.3 us
  transfers between devices with their start and end apart: 64, of which 64 were waited for; matrix products, arithmetic and copies ran while one was open for 0% of the time, Pallas kernels for 0%

commit v1 on v0

v1 whole, which is shorter than its diff:
```python
import jax
import jax.numpy as jnp
from jax import lax
from jax.experimental import pallas as pl
from jax.experimental.pallas import tpu as pltpu
from jax.sharding import PartitionSpec as P

MESH = pl.DeviceIdType.MESH
F32 = jnp.float32
BF16 = jnp.bfloat16
B = 320
V = 32
FACE = 80
LINES = 4


def split(value):
    high = value.astype(BF16)
    return high, (value - high.astype(F32)).astype(BF16)


def dot(a, b):
    return lax.dot_general(a, b, (((1,), (0,)), ((), ())), preferred_element_type=F32)


def dot_nt(a, b):
    return lax.dot_general(a, b, (((1,), (1,)), ((), ())), preferred_element_type=F32)


def product(a, b):
    return dot(a[0], b[0]) + dot(a[1], b[0]) + dot(a[0], b[1])


def apply(matrix, vectors):
    high, low = split(vectors)
    both = dot_nt(jnp.concatenate([high, low], 0), matrix[0])
    rows = vectors.shape[0]
    return both[:rows] + both[rows:] + dot_nt(high, matrix[1])


def apply_turned(matrix, vectors):
    high, low = split(vectors)
    both = dot(jnp.concatenate([high, low], 0), matrix[0])
    rows = vectors.shape[0]
    return both[:rows] + both[rows:] + dot(high, matrix[1])


def kernel(
    rhs_hbm, diag_hbm, lower_hbm, upper_hbm, proj_ref, list_ref, index_ref, angle_ref,
    out_ref, mortar_ref,
    diag, lower, upper, rhs,
    a_hl, g_hl, t_hl, w_hl, t_f, w_f, e_f, b_v, c_v, d_v,
    t_p, w_p, e_p, c_p, d_p,
    t_c, w_c, e_c, c_c, d_c,
    t_g, w_g, e_g, c_g, d_g,
    s_hop, x_hop, s_st, x_st, hop_st,
    s_in, x_in, s_0, s_1, u_0,
    tr_st, tr_all,
    load_sem, pair_s, pair_r, home_s, home_r, hop_s, hop_r,
    scat_s, sin_r, xin_r, core_s, tr_s, tr_r,
):
    axial = lax.axis_index("axial")
    theta = lax.axis_index("theta")
    core = lax.rem(axial, 2)
    x = lax.rem(axial // 2, 4)
    y = axial // 8
    other = 1 - core

    def at(row, chip, which):
        return ((row * 4 + chip) * 2 + which, theta)

    def remote(src, dst, send, recv, device):
        return pltpu.make_async_remote_copy(
            src_ref=src, dst_ref=dst, send_sem=send, recv_sem=recv,
            device_id=device, device_id_type=MESH,
        )

    barrier = pltpu.get_barrier_semaphore()

    def greet(device):
        pl.semaphore_signal(barrier, inc=1, device_id=device, device_id_type=MESH)

    for step in range(1, 8):
        greet((y * 8 + lax.rem(axial + step, 8), theta))
    greet((lax.rem(axial + 8, 32), theta))
    greet((lax.rem(axial + 24, 32), theta))
    for step in range(1, 4):
        greet((axial, lax.rem(theta + step, 4)))

    def load(which, line):
        src, dst = ((diag_hbm, diag), (lower_hbm, lower), (upper_hbm, upper), (rhs_hbm, rhs))[which]
        return pltpu.make_async_copy(src.at[line], dst.at[line], load_sem.at[which, line])

    order = [lax.rem(2 * other + i, 4) for i in range(4)]
    for line in order:
        load(0, line).start()
        load(1, line).start()
        load(3, line).start()
    for line in order:
        load(2, line).start()

    def whole(ref, *where):
        return ref[(*where, 0)], ref[(*where, 1)]

    def keep(ref, pair, *where):
        ref[(*where, 0)] = pair[0]
        ref[(*where, 1)] = pair[1]

    def first_maps(line):
        load(0, line).wait()
        load(1, line).wait()
        load(3, line).wait()
        for e in range(2):
            inverse = split(diag[line, e])
            keep(a_hl, split(product(inverse, split(lower[line, e]))), line, e)
            b_v[line, e] = apply(inverse, rhs[line, e])
        second = whole(a_hl, line, 1)
        across = product(second, whole(a_hl, line, 0))
        t_f[line] = across
        keep(t_hl, split(across), line)
        c_v[line] = b_v[line, 1] - apply(second, b_v[line, 0])

    def second_maps(line):
        load(2, line).wait()
        for e in range(2):
            keep(g_hl, split(product(split(diag[line, e]), split(upper[line, e]))), line, e)
        first = whole(g_hl, line, 0)
        across = product(first, whole(g_hl, line, 1))
        w_f[line] = across
        keep(w_hl, split(across), line)
        e_f[line] = -(
            a_hl[line, 0, 0].astype(F32) + a_hl[line, 0, 1].astype(F32)
        ) - product(first, whole(t_hl, line))
        d_v[line] = b_v[line, 0] - apply(first, c_v[line])

    def to_pair(kind, i):
        line = 2 * other + i
        src, dst = ((t_f, t_p), (c_v, c_p), (w_f, w_p), (e_f, e_p), (d_v, d_p))[kind]
        return remote(
            src.at[line], dst.at[i], pair_s.at[kind, i], pair_r.at[kind, i], at(y, x, other)
        )

    gathered = ((t_c, t_g), (c_c, c_g), (w_c, w_g), (e_c, e_g), (d_c, d_g))

    def to_home(kind, i, slot):
        src, dst = gathered[kind]
        return remote(
            src.at[i], dst.at[slot], home_s.at[kind, i], home_r.at[kind, slot],
            at(y, 2 * core + i, core),
        )

    def send_home(kinds, i):
        mine = x == 2 * core + i

        @pl.when(jnp.logical_not(mine))
        def _():
            for kind in kinds:
                to_home(kind, i, x).start()

        @pl.when(mine)
        def _():
            for kind in kinds:
                src, dst = gathered[kind]
                dst[x] = src[i]

    def pair_first(i, carry):
        first_maps(2 * other + i)

        @pl.when(i == 0)
        def _():
            pl.semaphore_wait(barrier, 12)

        to_pair(0, i).start()
        to_pair(1, i).start()
        return carry

    lax.fori_loop(0, 2, pair_first, 0)

    def pick(own, given):
        mine = core == 0
        return jnp.where(mine, own, given), jnp.where(mine, given, own)

    def own_first(i, carry):
        line = 2 * core + i
        first_maps(line)
        to_pair(0, i).wait_recv()
        to_pair(1, i).wait_recv()
        t_a, t_b = pick(t_f[line], t_p[i])
        c_a, c_b = pick(c_v[line], c_p[i])
        t_b = split(t_b)
        t_c[i] = product(t_b, split(t_a))
        c_c[i] = c_b + apply(t_b, c_a)
        send_home((0, 1), i)
        return carry

    lax.fori_loop(0, 2, own_first, 0)

    def pair_second(i, carry):
        second_maps(2 * other + i)
        for kind in (2, 3, 4):
            to_pair(kind, i).start()
        return carry

    lax.fori_loop(0, 2, pair_second, 0)

    def own_second(i, carry):
        line = 2 * core + i
        second_maps(line)
        for kind in (2, 3, 4):
            to_pair(kind, i).wait_recv()
        t_a, _ = pick(t_f[line], t_p[i])
        c_a, _ = pick(c_v[line], c_p[i])
        w_a, w_b = pick(w_f[line], w_p[i])
        e_a, e_b = pick(e_f[line], e_p[i])
        d_a, d_b = pick(d_v[line], d_p[i])
        w_a = split(w_a)
        e_b = split(e_b)
        w_c[i] = product(w_a, split(w_b))
        e_c[i] = e_a + product(w_a, split(product(e_b, split(t_a))))
        d_c[i] = d_a + apply(w_a, d_b + apply(e_b, c_a))
        send_home((2, 3, 4), i)
        return carry

    lax.fori_loop(0, 2, own_second, 0)

    is_home = x // 2 == core
    zero = jnp.zeros((V, B), F32)

    def arrived(kinds, slot):
        @pl.when(x != slot)
        def _():
            for kind in kinds:
                to_home(kind, 0, slot).wait_recv()

    def hop(way):
        src, dst, row = ((hop_st.at[0], s_hop, y + 1), (hop_st.at[1], x_hop, y - 1))[way]
        return remote(src, dst, hop_s.at[way], hop_r.at[way], at(row, x, core))

    def scatter(way, chip):
        src, dst, sem = ((s_st, s_in, sin_r), (x_st, x_in, xin_r))[way]
        return remote(src.at[chip], dst.at[x], scat_s.at[way, chip], sem.at[x], at(y, chip, way))

    def spread(way, chip, value):
        src, dst = ((s_st, s_in), (x_st, x_in))[way]
        src[chip] = value
        mine = jnp.logical_and(x == chip, core == way)

        @pl.when(jnp.logical_not(mine))
        def _():
            scatter(way, chip).start()

        @pl.when(mine)
        def _():
            dst[x] = value

    def home_forward():
        @pl.when(y == 0)
        def _():
            s_hop[...] = zero

        @pl.when(y > 0)
        def _():
            hop(0).wait_recv()

        state = s_hop[...]
        for chip in range(4):
            arrived((0, 1), chip)
            spread(0, chip, state)
            state = c_g[chip] + apply_turned(split(t_g[chip].T), state)
        hop_st[0] = state

        @pl.when(y < 3)
        def _():
            hop(0).start()

        for chip in range(4):
            arrived((3, 4), chip)
            d_g[chip] = d_g[chip] + apply(split(e_g[chip]), s_st[chip])

    def home_backward():
        @pl.when(y == 3)
        def _():
            x_hop[...] = zero

        @pl.when(y < 3)
        def _():
            hop(1).wait_recv()

        state = x_hop[...]
        for chip in (3, 2, 1, 0):
            arrived((2,), chip)
            spread(1, chip, state)
            state = d_g[chip] + apply_turned(split(w_g[chip].T), state)
        hop_st[1] = state

        @pl.when(y > 0)
        def _():
            hop(1).start()

    def to_core(line):
        forward = remote(
            s_1.at[line], s_in.at[line], core_s.at[line], sin_r.at[line], at(y, x, other)
        )
        back = remote(
            out_ref.at[line, 0], x_in.at[line], core_s.at[line], xin_r.at[line], at(y, x, other)
        )
        return forward, back

    def wait_state(line):
        mine = jnp.logical_and(is_home, jnp.logical_and(x == line, core == 0))

        @pl.when(jnp.logical_not(mine))
        def _():
            to_core(line)[0].wait_recv()

    def wait_solution(line):
        mine = jnp.logical_and(is_home, jnp.logical_and(x == line, core == 1))

        @pl.when(jnp.logical_not(mine))
        def _():
            to_core(line)[1].wait_recv()

    def finish_forward():
        for line in range(LINES):
            wait_state(line)
            s_1[line] = c_v[line] + apply(whole(t_hl, line), s_in[line])

            @pl.when(core == 0)
            def _():
                to_core(line)[0].start()

        for line in range(LINES):
            s_0[line] = b_v[line, 0] - apply(whole(a_hl, line, 0), s_in[line])
            u_0[line] = s_0[line] - apply(whole(g_hl, line, 0), s_1[line])

    def solve_first(line):
        out_ref[line, 0] = u_0[line] + apply(whole(w_hl, line), x_in[line])

    def solve_last(line):
        value = s_1[line] - apply(whole(g_hl, line, 1), x_in[line])
        out_ref[line, 1] = value
        tr_st[line] = value[:, B - FACE :]

    def to_theta(step):
        return remote(
            tr_st, tr_all.at[pl.ds(4 * theta, 4)], tr_s.at[step], tr_r.at[step],
            (axial, lax.rem(theta + step, 4)),
        )

    @pl.when(is_home)
    def _():
        home_forward()

    @pl.when(jnp.logical_and(is_home, y == 3))
    def _():
        home_backward()

    finish_forward()

    @pl.when(jnp.logical_and(is_home, y < 3))
    def _():
        home_backward()

    @pl.when(core == 1)
    def _():
        for line in range(LINES):
            wait_solution(line)
            solve_first(line)
            to_core(line)[1].start()
        for line in range(LINES):
            solve_last(line)

    @pl.when(core == 0)
    def _():
        for line in range(LINES):
            wait_solution(line)
            solve_last(line)

    for step in range(1, 4):
        to_theta(step).start()
    tr_all[pl.ds(4 * theta, 4)] = tr_st[...]

    @pl.when(core == 0)
    def _():
        for line in range(LINES):
            solve_first(line)

    for step in range(1, 4):
        to_theta(step).wait_recv()

    for face in range(LINES):
        total = jnp.zeros((V, FACE), F32)
        for k in range(2):
            source = lax.rem(list_ref[face, k] + angle_ref[0], 16)
            total += apply(split(proj_ref[index_ref[face, k]]), tr_all[source])
        mortar_ref[face] = total

    for i in range(2):
        mine = x == 2 * core + i
        for kind in range(5):
            to_pair(kind, i).wait_send()

            @pl.when(jnp.logical_not(mine))
            def _():
                to_home(kind, i, x).wait_send()

    @pl.when(is_home)
    def _():
        for way in range(2):
            for chip in range(4):
                mine = jnp.logical_and(x == chip, core == way)

                @pl.when(jnp.logical_not(mine))
                def _():
                    scatter(way, chip).wait_send()

        @pl.when(y < 3)
        def _():
            hop(0).wait_send()

        @pl.when(y > 0)
        def _():
            hop(1).wait_send()

    for line in range(LINES):
        @pl.when(core == 0)
        def _():
            to_core(line)[0].wait_send()

        @pl.when(core == 1)
        def _():
            to_core(line)[1].wait_send()

    for step in range(1, 4):
        to_theta(step).wait_send()


def local(rhs, diag, lower, upper, proj, intersections, index, angle):
    def mats(*lead, kind=F32):
        return pltpu.VMEM((*lead, B, B), kind)

    def vecs(*lead):
        return pltpu.VMEM((*lead, V, B), F32)

    def sems(*shape):
        return pltpu.SemaphoreType.DMA(shape)

    anywhere = pl.BlockSpec(memory_space=pl.ANY)
    vmem = pl.BlockSpec(memory_space=pltpu.VMEM)
    smem = pl.BlockSpec(memory_space=pltpu.SMEM)
    result, mortar = pl.pallas_call(
        kernel,
        out_shape=(
            jax.ShapeDtypeStruct((LINES, 2, V, B), F32),
            jax.ShapeDtypeStruct((LINES, V, FACE), F32),
        ),
        in_specs=[anywhere] * 4 + [vmem] + [smem] * 3,
        out_specs=(vmem, vmem),
        scratch_shapes=[
            mats(4, 2), mats(4, 2), mats(4, 2), vecs(4, 2),
            mats(4, 2, 2, kind=BF16), mats(4, 2, 2, kind=BF16), mats(4, 2, kind=BF16), mats(4, 2, kind=BF16),
            mats(4), mats(4), mats(4), vecs(4, 2), vecs(4), vecs(4),
            mats(2), mats(2), mats(2), vecs(2), vecs(2),
            mats(2), mats(2), mats(2), vecs(2), vecs(2),
            mats(4), mats(4), mats(4), vecs(4), vecs(4),
            vecs(), vecs(), vecs(4), vecs(4), vecs(2),
            vecs(4), vecs(4), vecs(4), vecs(4), vecs(4),
            pltpu.VMEM((4, V, FACE), F32), pltpu.VMEM((16, V, FACE), F32),
            sems(4, 4), sems(5, 2), sems(5, 2), sems(5, 2), sems(5, 4), sems(2), sems(2),
            sems(2, 4), sems(4), sems(4), sems(4), sems(4), sems(4),
        ],
        compiler_params=pltpu.CompilerParams(
            collective_id=0, has_side_effects=True, vmem_limit_bytes=60 * 2**20
        ),
        cost_estimate=pl.CostEstimate(flops=10**10, bytes_accessed=10**7, transcendentals=0),
    )(rhs, diag, lower, upper, proj, intersections, index, angle)
    return result, mortar.reshape(1, LINES, V * FACE)


def solution(mesh):
    line = P("theta", "axial", None, None)
    return jax.shard_map(
        local,
        mesh=mesh,
        in_specs=(line, line, line, line, P(), P("theta", None), P("theta", None), P()),
        out_specs=(line, P("axial", "theta", None)),
        check_vma=False,
    )
```

time: 1240 us -> 91.7 us (0.07)
  waiting for transfers between devices: 798 us -> 0 us
  starting transfers between devices: 343 us -> 0 us
  Pallas kernels: 0 us -> 83.8 us
  local copies, waits for them, and re-layouts: 49.3 us -> 6.01 us
  matrix products: 27.6 us -> 0 us
    ppermute x64 -> x0, waiting for transfers between devices: 798 us -> none  [shifted(): lax.ppermute(value, axis, [(source, source + steps) for source in range(f...]
    ppermute x64 -> x0, starting transfers between devices: 343 us -> none  [shifted(): lax.ppermute(value, axis, [(source, source + steps) for source in range(f...]
    pallas_call x0 -> x1, Pallas kernels: none -> 83.8 us  [local(): pl.pallas_call(kernel, out_shape=(jax.ShapeDtypeStruct((LINES, 2, V, B),...]
    another operation x66 -> x0, local copies, waits for them, and re-layouts: 42.9 us -> none
    dot_general x11 -> x0, matrix products: 27.6 us -> none  [the longest x8 26.3 us: product(): jnp.einsum('lbc,lvc->lvb', blocks, vectors, precision=lax.Precision.HIGHEST)]
  transfers between devices with their start and end apart: 64 -> 0, of which waited for: 64 -> 0; matrix products, arithmetic and copies ran while one was open for 0% -> 0% of each run, Pallas kernels for 0% -> 0%
where the time goes in v1:
time: 91.7 us; the launch traced here: 91.1 us
  Pallas kernels  83.8 us (91%)
  local copies, waits for them, and re-layouts  6.01 us (7%)
  between operations  1.29 us (1%)
    pallas_call x1, Pallas kernels, local(): pl.pallas_call(kernel, out_shape=(jax.ShapeDtypeStruct((LINES, 2, V, B),...  83.8 us
    unnamed x3, local copies, waits for them, and re-layouts  4.44 us

profile of v1, /device:TPU:1, one launch (start us, length us, event | category | flops | bytes accessed | tf_op | source)
XLA Modules:
  0.0 91.1 jit_solution(17341169777946664834)
XLA Ops:
  1.3 1.3 %copy.10.list_ref = s32[4,2]{1,0:T(4,128)} copy(s32[4,2]{0,1:T(2,128)} %param.13) | data formatting | bytes 64 | tf_op args[5]
  2.6 1.3 %copy.11.index_ref = s32[4,2]{1,0:T(4,128)} copy(s32[4,2]{0,1:T(2,128)} %param.14) | data formatting | bytes 64 | tf_op args[6]
  3.9 83.8 %shard_map.95 = (f32[4,2,32,320]{3,2,1,0:T(8,128)}, f32[4,32,80]{2,1,0:T(8,128)}) custom-call(f32[4,2,32,320]{3,2,1,0:T(8,128)} %rhs_hbm.1, f32[4,2,320,320]{3,2,1,0:T(8,128)} %diag_hbm.1, f32[4,2,320,320]{3,2,1,0:T(8,128)} %lower_hbm.1, f32[4,2,320,320]{3,2,1,0:T(8,128)} %upper_hbm.1, f32[16,80,80]{2,1,0:T(8,128)} %proj_ref.1, s32[4,2]{1,0:T(4,128)} %copy.10.list_ref, ...), custom_call_target="tpu_custom_call" | custom-call | flops 10000000000 | bytes 10000000 | tf_op jit(solution)/shard_map/pallas_call | solution.py:451
  87.7 1.6 %reshape.7 = f32[1,4,2560]{2,1,0:T(4,128)} reshape(f32[4,32,80]{2,1,0:T(8,128)} %get-tuple-element.5) | data formatting | bytes 81920 | tf_op jit(solution)/shard_map/reshape | solution.py:477
  89.3 1.8 %copy.14 = f32[4,2,32,320]{3,2,1,0:T(8,128)} copy(f32[4,2,32,320]{3,2,1,0:T(8,128)} %get-tuple-element.8) | data formatting | bytes 655360

commit v2 on v1

--- a/solution.py
+++ b/solution.py
@@ -45,19 +45,33 @@
     return both[:rows] + both[rows:] + dot(high, matrix[1])
 
 
+def packed(value):
+    rest = value[:, 256:]
+    return jnp.concatenate(
+        [value[:, :128], value[:, 128:256], jnp.concatenate([rest[:160], rest[160:]], 1)], 0
+    )
+
+
+def unpacked(value):
+    rest = value[640:]
+    return jnp.concatenate(
+        [value[:320], value[320:640], jnp.concatenate([rest[:, :64], rest[:, 64:]], 0)], 1
+    )
+
+
 def kernel(
     rhs_hbm, diag_hbm, lower_hbm, upper_hbm, proj_ref, list_ref, index_ref, angle_ref,
     out_ref, mortar_ref,
     diag, lower, upper, rhs,
     a_hl, g_hl, t_hl, w_hl, t_f, w_f, e_f, b_v, c_v, d_v,
     t_p, w_p, e_p, c_p, d_p,
-    t_c, w_c, e_c, c_c, d_c,
-    t_g, w_g, e_g, c_g, d_g,
+    t_c, w_c, e_hl, c_c, d_c,
+    t_g, w_g, c_g, d_g, turned, s_chip,
     s_hop, x_hop, s_st, x_st, hop_st,
     s_in, x_in, s_0, s_1, u_0,
     tr_st, tr_all,
     load_sem, pair_s, pair_r, home_s, home_r, hop_s, hop_r,
-    scat_s, sin_r, xin_r, core_s, tr_s, tr_r,
+    scat_s, sin_r, xin_r, core_s, tr_s, tr_r, chip_s, chip_r,
 ):
     axial = lax.axis_index("axial")
     theta = lax.axis_index("theta")
@@ -91,10 +105,11 @@
         src, dst = ((diag_hbm, diag), (lower_hbm, lower), (upper_hbm, upper), (rhs_hbm, rhs))[which]
         return pltpu.make_async_copy(src.at[line], dst.at[line], load_sem.at[which, line])
 
-    order = [lax.rem(2 * other + i, 4) for i in range(4)]
+    order = [2 * other, 2 * core, 2 * other + 1, 2 * core + 1]
     for line in order:
         load(0, line).start()
         load(1, line).start()
+    for line in order:
         load(3, line).start()
     for line in order:
         load(2, line).start()
@@ -109,25 +124,29 @@
     def first_maps(line):
         load(0, line).wait()
         load(1, line).wait()
-        load(3, line).wait()
         for e in range(2):
             inverse = split(diag[line, e])
             keep(a_hl, split(product(inverse, split(lower[line, e]))), line, e)
-            b_v[line, e] = apply(inverse, rhs[line, e])
-        second = whole(a_hl, line, 1)
-        across = product(second, whole(a_hl, line, 0))
+        across = product(whole(a_hl, line, 1), whole(a_hl, line, 0))
         t_f[line] = across
         keep(t_hl, split(across), line)
-        c_v[line] = b_v[line, 1] - apply(second, b_v[line, 0])
+
+    def first_vectors(line):
+        load(3, line).wait()
+        for e in range(2):
+            b_v[line, e] = apply(split(diag[line, e]), rhs[line, e])
+        c_v[line] = b_v[line, 1] - apply(whole(a_hl, line, 1), b_v[line, 0])
 
     def second_maps(line):
         load(2, line).wait()
         for e in range(2):
             keep(g_hl, split(product(split(diag[line, e]), split(upper[line, e]))), line, e)
-        first = whole(g_hl, line, 0)
-        across = product(first, whole(g_hl, line, 1))
+        across = product(whole(g_hl, line, 0), whole(g_hl, line, 1))
         w_f[line] = across
         keep(w_hl, split(across), line)
+
+    def third_maps(line):
+        first = whole(g_hl, line, 0)
         e_f[line] = -(
             a_hl[line, 0, 0].astype(F32) + a_hl[line, 0, 1].astype(F32)
         ) - product(first, whole(t_hl, line))
@@ -140,17 +159,17 @@
             src.at[line], dst.at[i], pair_s.at[kind, i], pair_r.at[kind, i], at(y, x, other)
         )
 
-    gathered = ((t_c, t_g), (c_c, c_g), (w_c, w_g), (e_c, e_g), (d_c, d_g))
+    gathered = ((t_c, t_g), (c_c, c_g), (w_c, w_g), None, (d_c, d_g))
 
     def to_home(kind, i, slot):
         src, dst = gathered[kind]
         return remote(
             src.at[i], dst.at[slot], home_s.at[kind, i], home_r.at[kind, slot],
-            at(y, 2 * core + i, core),
+            at(y, 2 * core + i, 1),
         )
 
     def send_home(kinds, i):
-        mine = x == 2 * core + i
+        mine = jnp.logical_and(x == 2 * core + i, core == 1)
 
         @pl.when(jnp.logical_not(mine))
         def _():
@@ -163,7 +182,7 @@
                 src, dst = gathered[kind]
                 dst[x] = src[i]
 
-    def pair_first(i, carry):
+    def both_first(i, carry):
         first_maps(2 * other + i)
 
         @pl.when(i == 0)
@@ -171,131 +190,191 @@
             pl.semaphore_wait(barrier, 12)
 
         to_pair(0, i).start()
-        to_pair(1, i).start()
-        return carry
-
-    lax.fori_loop(0, 2, pair_first, 0)
+        first_maps(2 * core + i)
+        return carry
+
+    lax.fori_loop(0, 2, both_first, 0)
 
     def pick(own, given):
         mine = core == 0
         return jnp.where(mine, own, given), jnp.where(mine, given, own)
 
-    def own_first(i, carry):
+    def chip_first(i, carry):
+        to_pair(0, i).wait_recv()
+        t_a, t_b = pick(t_f[2 * core + i], t_p[i])
+        t_c[i] = packed(product(split(t_b), split(t_a)))
+        send_home((0,), i)
+        return carry
+
+    lax.fori_loop(0, 2, chip_first, 0)
+
+    def pair_vectors(i, carry):
+        first_vectors(2 * other + i)
+        to_pair(1, i).start()
+        return carry
+
+    lax.fori_loop(0, 2, pair_vectors, 0)
+
+    def own_vectors(i, carry):
         line = 2 * core + i
-        first_maps(line)
-        to_pair(0, i).wait_recv()
+        first_vectors(line)
         to_pair(1, i).wait_recv()
-        t_a, t_b = pick(t_f[line], t_p[i])
+        _, t_b = pick(t_f[line], t_p[i])
         c_a, c_b = pick(c_v[line], c_p[i])
-        t_b = split(t_b)
-        t_c[i] = product(t_b, split(t_a))
-        c_c[i] = c_b + apply(t_b, c_a)
-        send_home((0, 1), i)
-        return carry
-
-    lax.fori_loop(0, 2, own_first, 0)
+        c_c[i] = c_b + apply(split(t_b), c_a)
+        send_home((1,), i)
+        return carry
+
+    lax.fori_loop(0, 2, own_vectors, 0)
+
+    is_home = core == 1
+    zero = jnp.zeros((V, B), F32)
+
+    def arrived(kinds, slot):
+        @pl.when(jnp.logical_not(jnp.logical_and(x == slot, x // 2 == 1)))
+        def _():
+            for kind in kinds:
+                to_home(kind, 0, slot).wait_recv()
+
+    def hop(way):
+        src, dst, row = ((hop_st.at[0], s_hop, y + 1), (hop_st.at[1], x_hop, y - 1))[way]
+        return remote(src, dst, hop_s.at[way], hop_r.at[way], at(row, x, core))
+
+    def scatter(way, chip):
+        src, dst, sem = ((s_st, s_in, sin_r), (x_st, x_in, xin_r))[way]
+        return remote(src.at[chip], dst.at[x], scat_s.at[way, chip], sem.at[x], at(y, chip, way))
+
+    def to_chip(chip):
+        return remote(
+            s_st.at[chip], s_chip.at[jnp.maximum(x - 2, 0)], chip_s.at[chip],
+            chip_r.at[jnp.maximum(x - 2, 0)], at(y, chip, 1),
+        )
+
+    def spread(way):
+        for chip in range(4):
+            src, dst = ((s_st, s_in), (x_st, x_in))[way]
+            mine = jnp.logical_and(x == chip, core == way)
+
+            @pl.when(jnp.logical_not(mine))
+            def _():
+                scatter(way, chip).start()
+
+            @pl.when(mine)
+            def _():
+                dst[x] = src[chip]
+
+    def home_forward():
+        for chip in range(4):
+            arrived((0, 1), chip)
+            keep(turned, split(unpacked(t_g[chip]).T), chip)
+
+        @pl.when(y == 0)
+        def _():
+            s_hop[...] = zero
+
+        @pl.when(y > 0)
+        def _():
+            hop(0).wait_recv()
+
+        state = s_hop[...]
+        for chip in range(4):
+            s_st[chip] = state
+            state = c_g[chip] + apply_turned(whole(turned, chip), state)
+        hop_st[0] = state
+
+        @pl.when(y < 3)
+        def _():
+            hop(0).start()
+
+        spread(0)
+        for chip in range(4):
+            @pl.when(jnp.logical_and(x > 1, x != chip))
+            def _():
+                to_chip(chip).start()
+
+            @pl.when(jnp.logical_and(x > 1, x == chip))
+            def _():
+                s_chip[x - 2] = s_st[chip]
+
+    def home_backward():
+        for chip in (3, 2, 1, 0):
+            arrived((2,), chip)
+            keep(turned, split(unpacked(w_g[chip]).T), chip)
+        for chip in (3, 2, 1, 0):
+            arrived((4,), chip)
+
+        @pl.when(y == 3)
+        def _():
+            x_hop[...] = zero
+
+        @pl.when(y < 3)
+        def _():
+            hop(1).wait_recv()
+
+        state = x_hop[...]
+        for chip in (3, 2, 1, 0):
+            x_st[chip] = state
+            state = d_g[chip] + apply_turned(whole(turned, chip), state)
+        hop_st[1] = state
+
+        @pl.when(y > 0)
+        def _():
+            hop(1).start()
+
+        spread(1)
+
+    def home_at(row, here):
+        @pl.when(jnp.logical_and(is_home, jnp.logical_and(y == row, here)))
+        def _():
+            home_forward()
 
     def pair_second(i, carry):
         second_maps(2 * other + i)
-        for kind in (2, 3, 4):
-            to_pair(kind, i).start()
+        to_pair(2, i).start()
         return carry
 
     lax.fori_loop(0, 2, pair_second, 0)
 
     def own_second(i, carry):
+        home_at(0, i == 1)
         line = 2 * core + i
         second_maps(line)
-        for kind in (2, 3, 4):
-            to_pair(kind, i).wait_recv()
+        to_pair(2, i).wait_recv()
+        w_a, w_b = pick(w_f[line], w_p[i])
+        w_c[i] = packed(product(split(w_a), split(w_b)))
+        send_home((2,), i)
+        return carry
+
+    lax.fori_loop(0, 2, own_second, 0)
+
+    def pair_third(i, carry):
+        home_at(1, i == 0)
+        third_maps(2 * other + i)
+        to_pair(3, i).start()
+        to_pair(4, i).start()
+        return carry
+
+    lax.fori_loop(0, 2, pair_third, 0)
+
+    def own_third(i, carry):
+        home_at(2, i == 1)
+        line = 2 * core + i
+        third_maps(line)
+        to_pair(3, i).wait_recv()
+        to_pair(4, i).wait_recv()
         t_a, _ = pick(t_f[line], t_p[i])
         c_a, _ = pick(c_v[line], c_p[i])
-        w_a, w_b = pick(w_f[line], w_p[i])
+        w_a, _ = pick(w_f[line], w_p[i])
         e_a, e_b = pick(e_f[line], e_p[i])
         d_a, d_b = pick(d_v[line], d_p[i])
         w_a = split(w_a)
         e_b = split(e_b)
-        w_c[i] = product(w_a, split(w_b))
-        e_c[i] = e_a + product(w_a, split(product(e_b, split(t_a))))
+        keep(e_hl, split(e_a + product(w_a, split(product(e_b, split(t_a))))), i)
         d_c[i] = d_a + apply(w_a, d_b + apply(e_b, c_a))
-        send_home((2, 3, 4), i)
-        return carry
-
-    lax.fori_loop(0, 2, own_second, 0)
-
-    is_home = x // 2 == core
-    zero = jnp.zeros((V, B), F32)
-
-    def arrived(kinds, slot):
-        @pl.when(x != slot)
-        def _():
-            for kind in kinds:
-                to_home(kind, 0, slot).wait_recv()
-
-    def hop(way):
-        src, dst, row = ((hop_st.at[0], s_hop, y + 1), (hop_st.at[1], x_hop, y - 1))[way]
-        return remote(src, dst, hop_s.at[way], hop_r.at[way], at(row, x, core))
-
-    def scatter(way, chip):
-        src, dst, sem = ((s_st, s_in, sin_r), (x_st, x_in, xin_r))[way]
-        return remote(src.at[chip], dst.at[x], scat_s.at[way, chip], sem.at[x], at(y, chip, way))
-
-    def spread(way, chip, value):
-        src, dst = ((s_st, s_in), (x_st, x_in))[way]
-        src[chip] = value
-        mine = jnp.logical_and(x == chip, core == way)
-
-        @pl.when(jnp.logical_not(mine))
-        def _():
-            scatter(way, chip).start()
-
-        @pl.when(mine)
-        def _():
-            dst[x] = value
-
-    def home_forward():
-        @pl.when(y == 0)
-        def _():
-            s_hop[...] = zero
-
-        @pl.when(y > 0)
-        def _():
-            hop(0).wait_recv()
-
-        state = s_hop[...]
-        for chip in range(4):
-            arrived((0, 1), chip)
-            spread(0, chip, state)
-            state = c_g[chip] + apply_turned(split(t_g[chip].T), state)
-        hop_st[0] = state
-
-        @pl.when(y < 3)
-        def _():
-            hop(0).start()
-
-        for chip in range(4):
-            arrived((3, 4), chip)
-            d_g[chip] = d_g[chip] + apply(split(e_g[chip]), s_st[chip])
-
-    def home_backward():
-        @pl.when(y == 3)
-        def _():
-            x_hop[...] = zero
-
-        @pl.when(y < 3)
-        def _():
-            hop(1).wait_recv()
-
-        state = x_hop[...]
-        for chip in (3, 2, 1, 0):
-            arrived((2,), chip)
-            spread(1, chip, state)
-            state = d_g[chip] + apply_turned(split(w_g[chip].T), state)
-        hop_st[1] = state
-
-        @pl.when(y > 0)
-        def _():
-            hop(1).start()
+        return carry
+
+    lax.fori_loop(0, 2, own_third, 0)
+    home_at(3, True)
 
     def to_core(line):
         forward = remote(
@@ -306,12 +385,24 @@
         )
         return forward, back
 
-    def wait_state(line):
-        mine = jnp.logical_and(is_home, jnp.logical_and(x == line, core == 0))
-
-        @pl.when(jnp.logical_not(mine))
-        def _():
-            to_core(line)[0].wait_recv()
+    def chip_backward():
+        for i in range(2):
+            @pl.when(core == 0)
+            def _():
+                to_core(i)[0].wait_recv()
+                d_c[i] = d_c[i] + apply(whole(e_hl, i), s_in[i])
+
+            @pl.when(core == 1)
+            def _():
+                @pl.when(x != 2 + i)
+                def _():
+                    remote(
+                        s_st.at[0], s_chip.at[i], chip_s.at[0], chip_r.at[i], at(y, x, other)
+                    ).wait_recv()
+
+                d_c[i] = d_c[i] + apply(whole(e_hl, i), s_chip[i])
+
+            send_home((4,), i)
 
     def wait_solution(line):
         mine = jnp.logical_and(is_home, jnp.logical_and(x == line, core == 1))
@@ -322,7 +413,10 @@
 
     def finish_forward():
         for line in range(LINES):
-            wait_state(line)
+            @pl.when(jnp.logical_or(core == 1, line > 1))
+            def _():
+                to_core(line)[0].wait_recv()
+
             s_1[line] = c_v[line] + apply(whole(t_hl, line), s_in[line])
 
             @pl.when(core == 0)
@@ -347,9 +441,7 @@
             (axial, lax.rem(theta + step, 4)),
         )
 
-    @pl.when(is_home)
-    def _():
-        home_forward()
+    chip_backward()
 
     @pl.when(jnp.logical_and(is_home, y == 3))
     def _():
@@ -391,18 +483,18 @@
     for face in range(LINES):
         total = jnp.zeros((V, FACE), F32)
         for k in range(2):
-            source = lax.rem(list_ref[face, k] + angle_ref[0], 16)
-            total += apply(split(proj_ref[index_ref[face, k]]), tr_all[source])
+            source = lax.rem(list_ref[k, face] + angle_ref[0], 16)
+            total += apply(split(proj_ref[index_ref[k, face]]), tr_all[source])
         mortar_ref[face] = total
 
     for i in range(2):
-        mine = x == 2 * core + i
+        mine = jnp.logical_and(x == 2 * core + i, core == 1)
         for kind in range(5):
             to_pair(kind, i).wait_send()
-
-            @pl.when(jnp.logical_not(mine))
-            def _():
-                to_home(kind, i, x).wait_send()
+            if kind != 3:
+                @pl.when(jnp.logical_not(mine))
+                def _():
+                    to_home(kind, i, x).wait_send()
 
     @pl.when(is_home)
     def _():
@@ -414,6 +506,11 @@
                 def _():
                     scatter(way, chip).wait_send()
 
+        for chip in range(4):
+            @pl.when(jnp.logical_and(x > 1, x != chip))
+            def _():
+                to_chip(chip).wait_send()
+
         @pl.when(y < 3)
         def _():
             hop(0).wait_send()
@@ -441,6 +538,9 @@
 
     def vecs(*lead):
         return pltpu.VMEM((*lead, V, B), F32)
+
+    def packs(*lead):
+        return pltpu.VMEM((*lead, 800, 128), F32)
 
     def sems(*shape):
         return pltpu.SemaphoreType.DMA(shape)
@@ -461,19 +561,19 @@
             mats(4, 2, 2, kind=BF16), mats(4, 2, 2, kind=BF16), mats(4, 2, kind=BF16), mats(4, 2, kind=BF16),
             mats(4), mats(4), mats(4), vecs(4, 2), vecs(4), vecs(4),
             mats(2), mats(2), mats(2), vecs(2), vecs(2),
-            mats(2), mats(2), mats(2), vecs(2), vecs(2),
-            mats(4), mats(4), mats(4), vecs(4), vecs(4),
+            packs(2), packs(2), mats(2, 2, kind=BF16), vecs(2), vecs(2),
+            packs(4), packs(4), vecs(4), vecs(4), mats(4, 2, kind=BF16), vecs(2),
             vecs(), vecs(), vecs(4), vecs(4), vecs(2),
             vecs(4), vecs(4), vecs(4), vecs(4), vecs(4),
             pltpu.VMEM((4, V, FACE), F32), pltpu.VMEM((16, V, FACE), F32),
             sems(4, 4), sems(5, 2), sems(5, 2), sems(5, 2), sems(5, 4), sems(2), sems(2),
-            sems(2, 4), sems(4), sems(4), sems(4), sems(4), sems(4),
+            sems(2, 4), sems(4), sems(4), sems(4), sems(4), sems(4), sems(4), sems(2),
         ],
         compiler_params=pltpu.CompilerParams(
             collective_id=0, has_side_effects=True, vmem_limit_bytes=60 * 2**20
         ),
         cost_estimate=pl.CostEstimate(flops=10**10, bytes_accessed=10**7, transcendentals=0),
-    )(rhs, diag, lower, upper, proj, intersections, index, angle)
+    )(rhs, diag, lower, upper, proj, intersections.T, index.T, angle)
     return result, mortar.reshape(1, LINES, V * FACE)
 
 

time: 91.7 us -> 71.1 us (0.78)
  Pallas kernels: 83.8 us -> 65.5 us
  local copies, waits for them, and re-layouts: 6.01 us -> 3.34 us
    pallas_call x1, Pallas kernels: 83.8 us -> 65.5 us  [local(): pl.pallas_call(kernel, out_shape=(jax.ShapeDtypeStruct((LINES, 2, V, B),...]
    unnamed x3 -> x1, local copies, waits for them, and re-layouts: 4.44 us -> 1.77 us
where the time goes in v2:
time: 71.1 us; the launch traced here: 70.1 us
  Pallas kernels  65.5 us (92%)
  local copies, waits for them, and re-layouts  3.34 us (5%)
  between operations  1.29 us (2%)
    pallas_call x1, Pallas kernels, local(): pl.pallas_call(kernel, out_shape=(jax.ShapeDtypeStruct((LINES, 2, V, B),...  65.5 us
    unnamed x1, local copies, waits for them, and re-layouts  1.77 us
    reshape x1, local copies, waits for them, and re-layouts, local(): return (result, mortar.reshape(1, LINES, V * FACE))  1.57 us

profile of v2, /device:TPU:1, one launch (start us, length us, event | category | flops | bytes accessed | tf_op | source)
XLA Modules:
  0.0 70.1 jit_solution(15955301797188121501)
XLA Ops:
  1.3 65.5 %shard_map.95 = (f32[4,2,32,320]{3,2,1,0:T(8,128)}, f32[4,32,80]{2,1,0:T(8,128)}) custom-call(f32[4,2,32,320]{3,2,1,0:T(8,128)} %rhs_hbm.1, f32[4,2,320,320]{3,2,1,0:T(8,128)} %diag_hbm.1, f32[4,2,320,320]{3,2,1,0:T(8,128)} %lower_hbm.1, f32[4,2,320,320]{3,2,1,0:T(8,128)} %upper_hbm.1, f32[16,80,80]{2,1,0:T(8,128)} %proj_ref.1, s32[2,4]{1,0:T(2,128)} %bitcast.2, ...), custom_call_target="tpu_custom_call" | custom-call | flops 10000000000 | bytes 10000000 | tf_op jit(solution)/shard_map/pallas_call | solution.py:551
  66.8 1.6 %reshape.7 = f32[1,4,2560]{2,1,0:T(4,128)} reshape(f32[4,32,80]{2,1,0:T(8,128)} %get-tuple-element.5) | data formatting | bytes 81920 | tf_op jit(solution)/shard_map/reshape | solution.py:577
  68.3 1.8 %copy.12 = f32[4,2,32,320]{3,2,1,0:T(8,128)} copy(f32[4,2,32,320]{3,2,1,0:T(8,128)} %get-tuple-element.8) | data formatting | bytes 655360

commit v3 on v2

--- a/solution.py
+++ b/solution.py
@@ -28,7 +28,11 @@
 
 
 def product(a, b):
-    return dot(a[0], b[0]) + dot(a[1], b[0]) + dot(a[0], b[1])
+    left = jnp.concatenate([a[0][:, 256:], a[1][:, 256:], a[0][:, 256:]], 1)
+    right = jnp.concatenate([b[0][256:], b[0][256:], b[1][256:]], 0)
+    high = a[0][:, :256]
+    main = dot(high, b[0][:256]) + dot(a[1][:, :256], b[0][:256]) + dot(high, b[1][:256])
+    return main + dot(left, right)
 
 
 def apply(matrix, vectors):
@@ -60,7 +64,7 @@
 
 
 def kernel(
-    rhs_hbm, diag_hbm, lower_hbm, upper_hbm, proj_ref, list_ref, index_ref, angle_ref,
+    rhs_hbm, diag_hbm, lower_hbm, upper_hbm, proj_hbm, list_hbm, index_hbm, angle_hbm,
     out_ref, mortar_ref,
     diag, lower, upper, rhs,
     a_hl, g_hl, t_hl, w_hl, t_f, w_f, e_f, b_v, c_v, d_v,
@@ -68,10 +72,10 @@
     t_c, w_c, e_hl, c_c, d_c,
     t_g, w_g, c_g, d_g, turned, s_chip,
     s_hop, x_hop, s_st, x_st, hop_st,
-    s_in, x_in, s_0, s_1, u_0,
-    tr_st, tr_all,
-    load_sem, pair_s, pair_r, home_s, home_r, hop_s, hop_r,
-    scat_s, sin_r, xin_r, core_s, tr_s, tr_r, chip_s, chip_r,
+    s_in, x_in, s_0, s_1, u_0, u_b, w_x, wb_hl,
+    tr_st, tr_all, proj_ref, list_ref, index_ref, angle_ref,
+    load_sem, table_sem, pair_s, pair_r, home_s, home_r, hop_s, hop_r,
+    scat_s, sin_r, xin_r, core_s, tr_s, tr_r, chip_s, chip_r, near_s, u_r, wx_s, wx_r,
 ):
     axial = lax.axis_index("axial")
     theta = lax.axis_index("theta")
@@ -105,7 +109,7 @@
         src, dst = ((diag_hbm, diag), (lower_hbm, lower), (upper_hbm, upper), (rhs_hbm, rhs))[which]
         return pltpu.make_async_copy(src.at[line], dst.at[line], load_sem.at[which, line])
 
-    order = [2 * other, 2 * core, 2 * other + 1, 2 * core + 1]
+    order = [2 * other, 2 * other + 1, 2 * core, 2 * core + 1]
     for line in order:
         load(0, line).start()
         load(1, line).start()
@@ -113,6 +117,14 @@
         load(3, line).start()
     for line in order:
         load(2, line).start()
+    tables = [
+        pltpu.make_async_copy(src, dst, table_sem.at[i])
+        for i, (src, dst) in enumerate(
+            ((proj_hbm, proj_ref), (list_hbm, list_ref), (index_hbm, index_ref), (angle_hbm, angle_ref))
+        )
+    ]
+    for table in tables:
+        table.start()
 
     def whole(ref, *where):
         return ref[(*where, 0)], ref[(*where, 1)]
@@ -182,18 +194,19 @@
                 src, dst = gathered[kind]
                 dst[x] = src[i]
 
-    def both_first(i, carry):
+    def pair_first(i, carry):
         first_maps(2 * other + i)
-
-        @pl.when(i == 0)
-        def _():
-            pl.semaphore_wait(barrier, 12)
-
+        return carry
+
+    def own_first(i, carry):
+        first_maps(2 * core + i)
+        return carry
+
+    lax.fori_loop(0, 2, pair_first, 0)
+    pl.semaphore_wait(barrier, 12)
+    for i in range(2):
         to_pair(0, i).start()
-        first_maps(2 * core + i)
-        return carry
-
-    lax.fori_loop(0, 2, both_first, 0)
+    lax.fori_loop(0, 2, own_first, 0)
 
     def pick(own, given):
         mine = core == 0
@@ -244,6 +257,12 @@
         src, dst, sem = ((s_st, s_in, sin_r), (x_st, x_in, xin_r))[way]
         return remote(src.at[chip], dst.at[x], scat_s.at[way, chip], sem.at[x], at(y, chip, way))
 
+    def scatter_near(chip):
+        return remote(x_st.at[chip], x_in.at[x], near_s.at[chip], xin_r.at[x], at(y, chip, 0))
+
+    def to_first(i):
+        return remote(w_f.at[2 + i], w_x.at[i], wx_s.at[i], wx_r.at[i], at(y, x, other))
+
     def to_chip(chip):
         return remote(
             s_st.at[chip], s_chip.at[jnp.maximum(x - 2, 0)], chip_s.at[chip],
@@ -321,6 +340,8 @@
         def _():
             hop(1).start()
 
+        for chip in range(4):
+            scatter_near(chip).start()
         spread(1)
 
     def home_at(row, here):
@@ -346,6 +367,12 @@
         return carry
 
     lax.fori_loop(0, 2, own_second, 0)
+
+    @pl.when(core == 1)
+    def _():
+        for i in range(2):
+            to_first(i).start()
+
 
     def pair_third(i, carry):
         home_at(1, i == 0)
@@ -381,7 +408,7 @@
             s_1.at[line], s_in.at[line], core_s.at[line], sin_r.at[line], at(y, x, other)
         )
         back = remote(
-            out_ref.at[line, 0], x_in.at[line], core_s.at[line], xin_r.at[line], at(y, x, other)
+            u_0.at[line], u_b.at[line], core_s.at[line], u_r.at[line], at(y, x, other)
         )
         return forward, back
 
@@ -409,7 +436,9 @@
 
         @pl.when(jnp.logical_not(mine))
         def _():
-            to_core(line)[1].wait_recv()
+            remote(
+                x_st.at[0], x_in.at[line], near_s.at[0], xin_r.at[line], at(y, x, other)
+            ).wait_recv()
 
     def finish_forward():
         for line in range(LINES):
@@ -426,6 +455,19 @@
         for line in range(LINES):
             s_0[line] = b_v[line, 0] - apply(whole(a_hl, line, 0), s_in[line])
             u_0[line] = s_0[line] - apply(whole(g_hl, line, 0), s_1[line])
+
+            @pl.when(core == 1)
+            def _():
+                to_core(line)[1].start()
+
+        @pl.when(core == 0)
+        def _():
+            for i in range(2):
+                keep(wb_hl, split(w_p[i]), i)
+                to_first(i).wait_recv()
+                keep(wb_hl, split(w_x[i]), 2 + i)
+            for line in range(LINES):
+                to_core(line)[1].wait_recv()
 
     def solve_first(line):
         out_ref[line, 0] = u_0[line] + apply(whole(w_hl, line), x_in[line])
@@ -457,29 +499,28 @@
     def _():
         for line in range(LINES):
             wait_solution(line)
-            solve_first(line)
-            to_core(line)[1].start()
-        for line in range(LINES):
             solve_last(line)
 
     @pl.when(core == 0)
     def _():
         for line in range(LINES):
             wait_solution(line)
+            x_in[line] = u_b[line] + apply(whole(wb_hl, line), x_in[line])
+        for line in range(LINES):
             solve_last(line)
 
     for step in range(1, 4):
         to_theta(step).start()
     tr_all[pl.ds(4 * theta, 4)] = tr_st[...]
 
-    @pl.when(core == 0)
-    def _():
-        for line in range(LINES):
-            solve_first(line)
+    for line in range(LINES):
+        solve_first(line)
 
     for step in range(1, 4):
         to_theta(step).wait_recv()
 
+    for table in tables:
+        table.wait()
     for face in range(LINES):
         total = jnp.zeros((V, FACE), F32)
         for k in range(2):
@@ -506,7 +547,11 @@
                 def _():
                     scatter(way, chip).wait_send()
 
+        for i in range(2):
+            to_first(i).wait_send()
         for chip in range(4):
+            scatter_near(chip).wait_send()
+
             @pl.when(jnp.logical_and(x > 1, x != chip))
             def _():
                 to_chip(chip).wait_send()
@@ -547,14 +592,13 @@
 
     anywhere = pl.BlockSpec(memory_space=pl.ANY)
     vmem = pl.BlockSpec(memory_space=pltpu.VMEM)
-    smem = pl.BlockSpec(memory_space=pltpu.SMEM)
     result, mortar = pl.pallas_call(
         kernel,
         out_shape=(
             jax.ShapeDtypeStruct((LINES, 2, V, B), F32),
             jax.ShapeDtypeStruct((LINES, V, FACE), F32),
         ),
-        in_specs=[anywhere] * 4 + [vmem] + [smem] * 3,
+        in_specs=[anywhere] * 8,
         out_specs=(vmem, vmem),
         scratch_shapes=[
             mats(4, 2), mats(4, 2), mats(4, 2), vecs(4, 2),
@@ -564,10 +608,12 @@
             packs(2), packs(2), mats(2, 2, kind=BF16), vecs(2), vecs(2),
             packs(4), packs(4), vecs(4), vecs(4), mats(4, 2, kind=BF16), vecs(2),
             vecs(), vecs(), vecs(4), vecs(4), vecs(2),
-            vecs(4), vecs(4), vecs(4), vecs(4), vecs(4),
+            vecs(4), vecs(4), vecs(4), vecs(4), vecs(4), vecs(4), mats(2), mats(4, 2, kind=BF16),
             pltpu.VMEM((4, V, FACE), F32), pltpu.VMEM((16, V, FACE), F32),
-            sems(4, 4), sems(5, 2), sems(5, 2), sems(5, 2), sems(5, 4), sems(2), sems(2),
-            sems(2, 4), sems(4), sems(4), sems(4), sems(4), sems(4), sems(4), sems(2),
+            pltpu.VMEM((16, FACE, FACE), F32), pltpu.SMEM((2, 4), jnp.int32), pltpu.SMEM((2, 4), jnp.int32),
+            pltpu.SMEM((1,), jnp.int32),
+            sems(4, 4), sems(4), sems(5, 2), sems(5, 2), sems(5, 2), sems(5, 4), sems(2), sems(2),
+            sems(2, 4), sems(4), sems(4), sems(4), sems(4), sems(4), sems(4), sems(2), sems(4), sems(4), sems(2), sems(2),
         ],
         compiler_params=pltpu.CompilerParams(
             collective_id=0, has_side_effects=True, vmem_limit_bytes=60 * 2**20

time: 71.1 us -> 68.9 us (0.969); the launches traced: 70.1 us -> 68.7 us
  Pallas kernels: 65.5 us -> 64 us
    pallas_call x1, Pallas kernels: 65.5 us -> 64 us  [local(): pl.pallas_call(kernel, out_shape=(jax.ShapeDtypeStruct((LINES, 2, V, B),...]
where the time goes in v3:
time: 68.9 us; the launch traced here: 68.7 us
  Pallas kernels  64 us (93%)
  local copies, waits for them, and re-layouts  3.34 us (5%)
  between operations  1.29 us (2%)
    pallas_call x1, Pallas kernels, local(): pl.pallas_call(kernel, out_shape=(jax.ShapeDtypeStruct((LINES, 2, V, B),...  64 us
    unnamed x1, local copies, waits for them, and re-layouts  1.77 us
    reshape x1, local copies, waits for them, and re-layouts, local(): return (result, mortar.reshape(1, LINES, V * FACE))  1.57 us

profile of v3, /device:TPU:1, one launch (start us, length us, event | category | flops | bytes accessed | tf_op | source)
XLA Modules:
  0.0 68.7 jit_solution(1950332069310513516)
XLA Ops:
  1.3 64.0 %shard_map.95 = (f32[4,2,32,320]{3,2,1,0:T(8,128)}, f32[4,32,80]{2,1,0:T(8,128)}) custom-call(f32[4,2,32,320]{3,2,1,0:T(8,128)} %rhs_hbm.1, f32[4,2,320,320]{3,2,1,0:T(8,128)} %diag_hbm.1, f32[4,2,320,320]{3,2,1,0:T(8,128)} %lower_hbm.1, f32[4,2,320,320]{3,2,1,0:T(8,128)} %upper_hbm.1, f32[16,80,80]{2,1,0:T(8,128)} %proj_hbm.1, s32[2,4]{1,0:T(2,128)} %bitcast.2, ...), custom_call_target="tpu_custom_call" | custom-call | flops 10000000000 | bytes 10000000 | tf_op jit(solution)/shard_map/pallas_call | solution.py:595
  65.3 1.6 %reshape.7 = f32[1,4,2560]{2,1,0:T(4,128)} reshape(f32[4,32,80]{2,1,0:T(8,128)} %get-tuple-element.5) | data formatting | bytes 81920 | tf_op jit(solution)/shard_map/reshape | solution.py:623
  66.9 1.8 %copy.12 = f32[4,2,32,320]{3,2,1,0:T(8,128)} copy(f32[4,2,32,320]{3,2,1,0:T(8,128)} %get-tuple-element.8) | data formatting | bytes 655360

commit v4 on v3

--- a/solution.py
+++ b/solution.py
@@ -44,9 +44,13 @@
 
 def apply_turned(matrix, vectors):
     high, low = split(vectors)
-    both = dot(jnp.concatenate([high, low], 0), matrix[0])
     rows = vectors.shape[0]
-    return both[:rows] + both[rows:] + dot(high, matrix[1])
+    both = jnp.concatenate([high, low], 0)
+    none = jnp.zeros((rows, 64), BF16)
+    left = jnp.concatenate([both[:, 256:], jnp.concatenate([high[:, 256:], none], 0)], 1)
+    right = jnp.concatenate([matrix[0][256:], matrix[1][256:]], 0)
+    main = dot(both[:, :256], matrix[0][:256]) + dot(left, right)
+    return main[:rows] + main[rows:] + dot(high[:, :256], matrix[1][:256])
 
 
 def packed(value):
@@ -475,7 +479,10 @@
     def solve_last(line):
         value = s_1[line] - apply(whole(g_hl, line, 1), x_in[line])
         out_ref[line, 1] = value
-        tr_st[line] = value[:, B - FACE :]
+
+    def trace(line):
+        face = g_hl[line, 1, 0, B - FACE :, :], g_hl[line, 1, 1, B - FACE :, :]
+        tr_st[line] = s_1[line][:, B - FACE :] - apply(face, x_in[line])
 
     def to_theta(step):
         return remote(
@@ -499,7 +506,7 @@
     def _():
         for line in range(LINES):
             wait_solution(line)
-            solve_last(line)
+            trace(line)
 
     @pl.when(core == 0)
     def _():
@@ -507,13 +514,14 @@
             wait_solution(line)
             x_in[line] = u_b[line] + apply(whole(wb_hl, line), x_in[line])
         for line in range(LINES):
-            solve_last(line)
+            trace(line)
 
     for step in range(1, 4):
         to_theta(step).start()
     tr_all[pl.ds(4 * theta, 4)] = tr_st[...]
 
     for line in range(LINES):
+        solve_last(line)
         solve_first(line)
 
     for step in range(1, 4):

time: 68.9 us -> 70.2 us (1.019)
  Pallas kernels: 64 us -> 65.3 us
    pallas_call x1, Pallas kernels: 64 us -> 65.3 us  [local(): pl.pallas_call(kernel, out_shape=(jax.ShapeDtypeStruct((LINES, 2, V, B),...]
where the time goes in v4:
time: 70.2 us; the launch traced here: 70 us
  Pallas kernels  65.3 us (93%)
  local copies, waits for them, and re-layouts  3.34 us (5%)
  between operations  1.29 us (2%)
    pallas_call x1, Pallas kernels, local(): pl.pallas_call(kernel, out_shape=(jax.ShapeDtypeStruct((LINES, 2, V, B),...  65.3 us
    unnamed x1, local copies, waits for them, and re-layouts  1.77 us
    reshape x1, local copies, waits for them, and re-layouts, local(): return (result, mortar.reshape(1, LINES, V * FACE))  1.57 us

profile of v4, /device:TPU:1, one launch (start us, length us, event | category | flops | bytes accessed | tf_op | source)
XLA Modules:
  0.0 70.0 jit_solution(10481351852345159791)
XLA Ops:
  1.3 65.3 %shard_map.95 = (f32[4,2,32,320]{3,2,1,0:T(8,128)}, f32[4,32,80]{2,1,0:T(8,128)}) custom-call(f32[4,2,32,320]{3,2,1,0:T(8,128)} %rhs_hbm.1, f32[4,2,320,320]{3,2,1,0:T(8,128)} %diag_hbm.1, f32[4,2,320,320]{3,2,1,0:T(8,128)} %lower_hbm.1, f32[4,2,320,320]{3,2,1,0:T(8,128)} %upper_hbm.1, f32[16,80,80]{2,1,0:T(8,128)} %proj_hbm.1, s32[2,4]{1,0:T(2,128)} %bitcast.2, ...), custom_call_target="tpu_custom_call" | custom-call | flops 10000000000 | bytes 10000000 | tf_op jit(solution)/shard_map/pallas_call | solution.py:603
  66.6 1.6 %reshape.7 = f32[1,4,2560]{2,1,0:T(4,128)} reshape(f32[4,32,80]{2,1,0:T(8,128)} %get-tuple-element.5) | data formatting | bytes 81920 | tf_op jit(solution)/shard_map/reshape | solution.py:631
  68.2 1.8 %copy.12 = f32[4,2,32,320]{3,2,1,0:T(8,128)} copy(f32[4,2,32,320]{3,2,1,0:T(8,128)} %get-tuple-element.8) | data formatting | bytes 655360

commit v5 on v3

--- a/solution.py
+++ b/solution.py
@@ -269,18 +269,27 @@
             chip_r.at[jnp.maximum(x - 2, 0)], at(y, chip, 1),
         )
 
-    def spread(way):
-        for chip in range(4):
-            src, dst = ((s_st, s_in), (x_st, x_in))[way]
-            mine = jnp.logical_and(x == chip, core == way)
-
-            @pl.when(jnp.logical_not(mine))
-            def _():
-                scatter(way, chip).start()
-
-            @pl.when(mine)
-            def _():
-                dst[x] = src[chip]
+    def send_state(chip):
+        @pl.when(jnp.logical_and(x > 1, x != chip))
+        def _():
+            to_chip(chip).start()
+
+        @pl.when(jnp.logical_and(x > 1, x == chip))
+        def _():
+            s_chip[x - 2] = s_st[chip]
+
+        scatter(0, chip).start()
+
+    def send_solution(chip):
+        scatter_near(chip).start()
+
+        @pl.when(x != chip)
+        def _():
+            scatter(1, chip).start()
+
+        @pl.when(x == chip)
+        def _():
+            x_in[x] = x_st[chip]
 
     def home_forward():
         for chip in range(4):
@@ -298,22 +307,19 @@
         state = s_hop[...]
         for chip in range(4):
             s_st[chip] = state
+
+            @pl.when(y == 3)
+            def _():
+                send_state(chip)
+
             state = c_g[chip] + apply_turned(whole(turned, chip), state)
         hop_st[0] = state
 
         @pl.when(y < 3)
         def _():
             hop(0).start()
-
-        spread(0)
-        for chip in range(4):
-            @pl.when(jnp.logical_and(x > 1, x != chip))
-            def _():
-                to_chip(chip).start()
-
-            @pl.when(jnp.logical_and(x > 1, x == chip))
-            def _():
-                s_chip[x - 2] = s_st[chip]
+            for chip in range(4):
+                send_state(chip)
 
     def home_backward():
         for chip in (3, 2, 1, 0):
@@ -333,16 +339,19 @@
         state = x_hop[...]
         for chip in (3, 2, 1, 0):
             x_st[chip] = state
+
+            @pl.when(y == 0)
+            def _():
+                send_solution(chip)
+
             state = d_g[chip] + apply_turned(whole(turned, chip), state)
         hop_st[1] = state
 
         @pl.when(y > 0)
         def _():
             hop(1).start()
-
-        for chip in range(4):
-            scatter_near(chip).start()
-        spread(1)
+            for chip in (3, 2, 1, 0):
+                send_solution(chip)
 
     def home_at(row, here):
         @pl.when(jnp.logical_and(is_home, jnp.logical_and(y == row, here)))

time: 68.9 us -> 69.1 us (level)
  no operation moved by 1% of the time
where the time goes in v5:
time: 69.1 us; the launch traced here: 68.7 us
  Pallas kernels  64.1 us (93%)
  local copies, waits for them, and re-layouts  3.34 us (5%)
  between operations  1.29 us (2%)
    pallas_call x1, Pallas kernels, local(): pl.pallas_call(kernel, out_shape=(jax.ShapeDtypeStruct((LINES, 2, V, B),...  64.1 us
    unnamed x1, local copies, waits for them, and re-layouts  1.77 us
    reshape x1, local copies, waits for them, and re-layouts, local(): return (result, mortar.reshape(1, LINES, V * FACE))  1.57 us

profile of v5, /device:TPU:1, one launch (start us, length us, event | category | flops | bytes accessed | tf_op | source)
XLA Modules:
  0.0 68.7 jit_solution(7336958711933837785)
XLA Ops:
  1.3 64.1 %shard_map.95 = (f32[4,2,32,320]{3,2,1,0:T(8,128)}, f32[4,32,80]{2,1,0:T(8,128)}) custom-call(f32[4,2,32,320]{3,2,1,0:T(8,128)} %rhs_hbm.1, f32[4,2,320,320]{3,2,1,0:T(8,128)} %diag_hbm.1, f32[4,2,320,320]{3,2,1,0:T(8,128)} %lower_hbm.1, f32[4,2,320,320]{3,2,1,0:T(8,128)} %upper_hbm.1, f32[16,80,80]{2,1,0:T(8,128)} %proj_hbm.1, s32[2,4]{1,0:T(2,128)} %bitcast.2, ...), custom_call_target="tpu_custom_call" | custom-call | flops 10000000000 | bytes 10000000 | tf_op jit(solution)/shard_map/pallas_call | solution.py:604
  65.4 1.6 %reshape.7 = f32[1,4,2560]{2,1,0:T(4,128)} reshape(f32[4,32,80]{2,1,0:T(8,128)} %get-tuple-element.5) | data formatting | bytes 81920 | tf_op jit(solution)/shard_map/reshape | solution.py:632
  67.0 1.8 %copy.12 = f32[4,2,32,320]{3,2,1,0:T(8,128)} copy(f32[4,2,32,320]{3,2,1,0:T(8,128)} %get-tuple-element.8) | data formatting | bytes 655360

commit v6 on v5

--- a/solution.py
+++ b/solution.py
@@ -484,7 +484,10 @@
     def solve_last(line):
         value = s_1[line] - apply(whole(g_hl, line, 1), x_in[line])
         out_ref[line, 1] = value
-        tr_st[line] = value[:, B - FACE :]
+
+    def trace(line):
+        face = g_hl[line, 1, 0, B - FACE :, :], g_hl[line, 1, 1, B - FACE :, :]
+        tr_st[line] = s_1[line][:, B - FACE :] - apply(face, x_in[line])
 
     def to_theta(step):
         return remote(
@@ -508,7 +511,7 @@
     def _():
         for line in range(LINES):
             wait_solution(line)
-            solve_last(line)
+            trace(line)
 
     @pl.when(core == 0)
     def _():
@@ -516,13 +519,14 @@
             wait_solution(line)
             x_in[line] = u_b[line] + apply(whole(wb_hl, line), x_in[line])
         for line in range(LINES):
-            solve_last(line)
+            trace(line)
 
     for step in range(1, 4):
         to_theta(step).start()
     tr_all[pl.ds(4 * theta, 4)] = tr_st[...]
 
     for line in range(LINES):
+        solve_last(line)
         solve_first(line)
 
     for step in range(1, 4):

time: 69.1 us -> 69 us (level)
  no operation moved by 1% of the time
where the time goes in v6:
time: 69 us; the launch traced here: 68.8 us
  Pallas kernels  64.2 us (93%)
  local copies, waits for them, and re-layouts  3.34 us (5%)
  between operations  1.29 us (2%)
    pallas_call x1, Pallas kernels, local(): pl.pallas_call(kernel, out_shape=(jax.ShapeDtypeStruct((LINES, 2, V, B),...  64.2 us
    unnamed x1, local copies, waits for them, and re-layouts  1.77 us
    reshape x1, local copies, waits for them, and re-layouts, local(): return (result, mortar.reshape(1, LINES, V * FACE))  1.57 us

profile of v6, /device:TPU:1, one launch (start us, length us, event | category | flops | bytes accessed | tf_op | source)
XLA Modules:
  0.0 68.8 jit_solution(11273223322133631211)
XLA Ops:
  1.3 64.2 %shard_map.95 = (f32[4,2,32,320]{3,2,1,0:T(8,128)}, f32[4,32,80]{2,1,0:T(8,128)}) custom-call(f32[4,2,32,320]{3,2,1,0:T(8,128)} %rhs_hbm.1, f32[4,2,320,320]{3,2,1,0:T(8,128)} %diag_hbm.1, f32[4,2,320,320]{3,2,1,0:T(8,128)} %lower_hbm.1, f32[4,2,320,320]{3,2,1,0:T(8,128)} %upper_hbm.1, f32[16,80,80]{2,1,0:T(8,128)} %proj_hbm.1, s32[2,4]{1,0:T(2,128)} %bitcast.2, ...), custom_call_target="tpu_custom_call" | custom-call | flops 10000000000 | bytes 10000000 | tf_op jit(solution)/shard_map/pallas_call | solution.py:608
  65.5 1.6 %reshape.7 = f32[1,4,2560]{2,1,0:T(4,128)} reshape(f32[4,32,80]{2,1,0:T(8,128)} %get-tuple-element.5) | data formatting | bytes 81920 | tf_op jit(solution)/shard_map/reshape | solution.py:636
  67.1 1.8 %copy.12 = f32[4,2,32,320]{3,2,1,0:T(8,128)} copy(f32[4,2,32,320]{3,2,1,0:T(8,128)} %get-tuple-element.8) | data formatting | bytes 655360
